TPU v7x, 1024 devices: a whole 4x8x16 slice. The times are simulated.
1024 devices in a mesh: comp: 16 (over x, z_hi), tile: 64 (over z_lo, y, core).
Axes of the slice: x: 4, y: 8, z: 16 (z_hi: 4, z_lo: 4; z = z_hi * 4 + z_lo), core: 2. Of those that a mesh axis runs over, the one named last changes fastest.
Arguments:
- atmos_state: float32 [128, 1024, 128], P('comp', 'tile'), may hold values from -6 to 6
- wind_field: bfloat16 [2, 128, 1024, 128], P(None, 'comp', 'tile'), may hold values from -5 to 5
- ocean_height: float32 [512, 8192], P('comp', 'tile'), may hold values from -6 to 6
- ocean_potential: float32 [512, 8192], P('comp', 'tile'), may hold values from -6 to 6
- ocean_neighbors: int32 [6, 512, 8192], P(None, 'comp', 'tile'), may hold values from 0 to 4419, as said below
- ocean_coupling: float32 [6, 512, 8192], P(None, 'comp', 'tile'), may hold values from 0.1 to 0.5
- downward_source: int32 [16, 4096, 128], P('comp', 'tile'), may hold values from 0 to 127, as said below
- downward_target: int32 [16, 4096, 128], P('comp', 'tile'), may hold values from 0 to 4095, as said below
- downward_weight: float32 [16, 4096, 128], P('comp', 'tile'), may hold values from 0.3 to 1.2
- upward_source: int32 [16, 4096, 128], P('comp', 'tile'), may hold values from 0 to 4095, as said below
- upward_target: int32 [16, 4096, 128], P('comp', 'tile'), may hold values from 0 to 127, as said below
- upward_weight: float32 [16, 4096, 128], P('comp', 'tile'), may hold values from 0.05 to 0.3
Outputs:
- atmos_out: float32 [128, 1024, 128], P('comp', 'tile')
- height_out: float32 [512, 8192], P('comp', 'tile')
- potential_out: float32 [512, 8192], P('comp', 'tile')
- surface_flux: float32 [128, 1024], P('comp', 'tile')
Inputs may be any that keep to these rules, and one draw needn't show every extreme that they name: `ocean_neighbors`: the six entries of a cell are distinct and name the four cells beside it along the two dimensions and one of the two diagonal pairs. `downward_source`: within a row of devices the ocean's blocks are laid out differently from the atmosphere's, so the surface under one ocean block is spread over all devices of the row; band p of a device's local points (flat order, p * 8 * 16 // 64 onward, 2 of them) lies over row-peer p. Entries for peer p name points of band p. `downward_target`: entries from peer p name ocean cells of band p of the receiving device's cells (flat order, 64 of them from p * 32 * 2). `upward_source`: entries for peer p name ocean cells of band p of the sending device's cells (flat order, 64 of them from p * 32 * 2). `upward_target`: entries from peer p name surface points of band p of the receiving device's points (flat order, 2 of them from p * 8 * 16 // 64).
All inputs are finite; a program needn't handle non-finite values.
Results may differ from a plain program's by a relative error of at most 0.0003.
Values sent between devices are 32-bit elements; how exact they have to be, the bound alone decides.
A program may use at most 32 MiB of HBM per device.

v0:
```python
import jax
import jax.numpy as jnp
import numpy as np
from jax import lax
from jax.sharding import PartitionSpec as P

NP = 4
OX = 32
OY = 128
SUBSTEPS = 2
SUBCYCLES = 8


atmos_step = 0.05
viscosity = 0.05
ocean_step = 0.2
wave_speed = 1.0
friction = 0.05


def with_halo(block, sides, width):
    for axis, dim in sides:
        count = lax.axis_size(axis)
        forward = [(i, i + 1) for i in range(count - 1)]
        forward.append((count - 1, 0))
        backward = [(target, source) for source, target in forward]
        low = lax.ppermute(
            lax.slice_in_dim(block, block.shape[dim] - width, None, axis=dim), axis, forward
        )
        high = lax.ppermute(lax.slice_in_dim(block, 0, width, axis=dim), axis, backward)
        block = jnp.concatenate([low, block, high], axis=dim)
    return block


def gll_derivative():
    points = np.array([-1.0, -1.0 / np.sqrt(5.0), 1.0 / np.sqrt(5.0), 1.0])
    weights = np.array(
        [1.0 / np.prod([points[j] - points[k] for k in range(4) if k != j]) for j in range(4)]
    )
    matrix = np.zeros((4, 4))
    for i in range(4):
        for j in range(4):
            if i != j:
                matrix[i, j] = weights[j] / weights[i] / (points[i] - points[j])
        matrix[i, i] = -np.sum(matrix[i])
    return matrix


def along_first(values, matrix):
    extent_rows, extent_cols, levels = values.shape
    shaped = values.reshape(extent_rows // NP, NP, extent_cols, levels)
    result = jnp.einsum("ik,ekyl->eiyl", matrix, shaped, precision=lax.Precision.HIGHEST)
    return result.reshape(extent_rows, extent_cols, levels)


def along_second(values, matrix):
    extent_rows, extent_cols, levels = values.shape
    shaped = values.reshape(extent_rows, extent_cols // NP, NP, levels)
    result = jnp.einsum("ik,xekl->xeil", matrix, shaped, precision=lax.Precision.HIGHEST)
    return result.reshape(extent_rows, extent_cols, levels)


def tendency(atmos, wind_east, wind_north):
    first_order = gll_derivative()
    second_order = jnp.asarray(first_order @ first_order, jnp.float32)
    first_order = jnp.asarray(first_order, jnp.float32)
    slope_east = along_first(atmos, first_order)
    slope_north = along_second(atmos, first_order)
    curvature = along_first(atmos, second_order) + along_second(atmos, second_order)
    return viscosity * curvature - (wind_east * slope_east + wind_north * slope_north)


def pair_mean(values, after, before, axis):
    length = values.shape[axis]
    extent = [1] * values.ndim
    extent[axis] = length
    position = (jnp.arange(length, dtype=jnp.int32) % NP).reshape(extent)
    return jnp.where(
        position == NP - 1,
        0.5 * (values + after),
        jnp.where(position == 0, 0.5 * (values + before), values),
    )


def average_pairs(padded):
    across = pair_mean(padded[1:-1], padded[2:], padded[:-2], 0)
    return pair_mean(across[:, 1:-1], across[:, 2:], across[:, :-2], 1)


def stencil(neighbors, coupling):
    extent_rows, extent_cols = (neighbors.shape[1], neighbors.shape[2])
    row_local = (jnp.arange(extent_rows, dtype=jnp.int32) % OX)[None, :, None]
    col_local = (jnp.arange(extent_cols, dtype=jnp.int32) % OY)[None, None, :]
    offset_row = neighbors // (OY + 2) - 1 - row_local
    offset_col = neighbors % (OY + 2) - 1 - col_local
    offset_code = (offset_row + 1) * 3 + offset_col + 1
    layers = [jnp.sum(jnp.where(offset_code == o, coupling, 0.0), axis=0) for o in range(9)]
    layers[4] = layers[4] - jnp.sum(coupling, axis=0)
    return jnp.stack(layers)


def apply_inner(weights_nine, padded):
    inner_rows = padded.shape[0] - 2
    inner_cols = padded.shape[1] - 2
    summed = jnp.zeros((inner_rows, inner_cols), jnp.float32)
    for o in range(9):
        shifted = padded[o // 3 : o // 3 + inner_rows, o % 3 : o % 3 + inner_cols]
        summed = summed + weights_nine[o] * shifted
    return summed


def band_onehot(table, band):
    peers = table.shape[0]
    local_index = table - jnp.arange(peers, dtype=jnp.int32)[:, None] * band
    return (local_index[:, :, None] == jnp.arange(band, dtype=jnp.int32)[None, None, :]).astype(
        jnp.float32
    )


def pick_bands(values_flat, table):
    peers = table.shape[0]
    band = values_flat.shape[0] // peers
    bands = values_flat.reshape(peers, band)
    return jnp.einsum(
        "psk,pk->ps", band_onehot(table, band), bands, precision=lax.Precision.HIGHEST
    )


def place_bands(table, contribution, total):
    peers = table.shape[0]
    band = total // peers
    placed = jnp.einsum(
        "psk,ps->pk", band_onehot(table, band), contribution, precision=lax.Precision.HIGHEST
    )
    return placed.reshape(total)


def on_device(
    atmos_state,
    wind_field,
    ocean_height,
    ocean_potential,
    ocean_neighbors,
    ocean_coupling,
    downward_source,
    downward_target,
    downward_weight,
    upward_source,
    upward_target,
    upward_weight,
):
    atmos = atmos_state
    wind_east = wind_field[0].astype(jnp.float32)
    wind_north = wind_field[1].astype(jnp.float32)
    margin = NP * SUBSTEPS
    stacked = jnp.stack([atmos, wind_east, wind_north])
    extended = with_halo(stacked, (("comp", 1), ("tile", 2)), margin)
    grown = extended[0]
    for substep in range(SUBSTEPS):
        tendency_field = tendency(grown, extended[1], extended[2])
        padded = jnp.pad(tendency_field, ((1, 1), (1, 1), (0, 0)), mode="edge")
        grown = grown + atmos_step * average_pairs(padded)
    atmos = grown[margin:-margin, margin:-margin]
    node_count = atmos.shape[0] * atmos.shape[1]
    cell_count = ocean_height.shape[0] * ocean_height.shape[1]
    outgoing = pick_bands(atmos[:, :, -1].reshape(-1), downward_source[0]).reshape(-1)
    arrived = lax.all_to_all(outgoing, "tile", split_axis=0, concat_axis=0, tiled=True)
    arrived = arrived.reshape(downward_weight[0].shape)
    forcing = place_bands(downward_target[0], downward_weight[0] * arrived, cell_count)
    forcing = forcing.reshape(ocean_height.shape)
    weights_nine = stencil(ocean_neighbors, ocean_coupling)
    height = ocean_height
    potential = ocean_potential
    stacked = jnp.concatenate([height[None], potential[None], forcing[None], weights_nine], 0)
    extended = with_halo(stacked, (("comp", 1), ("tile", 2)), SUBCYCLES)
    height = extended[0]
    potential = extended[1]
    forcing = extended[2]
    weights_nine = extended[3:]
    for substep in range(SUBCYCLES):
        potential = (1.0 - friction) * potential + ocean_step * (wave_speed * height + forcing)
        weights_nine = weights_nine[:, 1:-1, 1:-1]
        height = height[1:-1, 1:-1] + ocean_step * apply_inner(weights_nine, potential)
        potential = potential[1:-1, 1:-1]
        forcing = forcing[1:-1, 1:-1]
    outgoing = pick_bands(height.reshape(-1), upward_source[0]).reshape(-1)
    arrived = lax.all_to_all(outgoing, "tile", split_axis=0, concat_axis=0, tiled=True)
    arrived = arrived.reshape(upward_weight[0].shape)
    surface_flux = place_bands(upward_target[0], upward_weight[0] * arrived, node_count)
    surface_flux = surface_flux.reshape(atmos.shape[0], atmos.shape[1])
    return (atmos, height, potential, surface_flux)


def solution(mesh):
    return jax.shard_map(
        on_device,
        mesh=mesh,
        in_specs=(
            P("comp", "tile", None),
            P(None, "comp", "tile", None),
            P("comp", "tile"),
            P("comp", "tile"),
            P(None, "comp", "tile"),
            P(None, "comp", "tile"),
            P("comp", "tile", None),
            P("comp", "tile", None),
            P("comp", "tile", None),
            P("comp", "tile", None),
            P("comp", "tile", None),
            P("comp", "tile", None),
        ),
        out_specs=(
            P("comp", "tile", None),
            P("comp", "tile"),
            P("comp", "tile"),
            P("comp", "tile"),
        ),
        check_vma=False,
    )
```

profile of v0, /device:TPU:1, one launch (start us, length us, event | category | flops | bytes accessed | tf_op | source)
XLA Modules:
  0.0 144.1 jit_solution(5346910016305697127)
XLA Ops:
  0.6 0.8 slice_convert_fusion.1
  1.4 0.9 pad_maximum_fusion.4
  2.3 11.5 %collective-permute-start = (f32[3,8,16,128]{3,2,1,0:T(8,128)S(1)}, f32[3,8,16,128]{3,2,1,0:T(8,128)S(1)}, u32[]{:S(2)}, u32[]{:S(2)}) collective-permute-start(f32[3,8,16,128]{3,2,1,0:T(8,128)S(1)} %pad_maximum_fusion.4), channel_id=1, source_target_pairs={{0,64},{64,128},{128,192},{192,256},{256,320},{320,384},{384,448},... | collective-permute-start | bytes 589832 | tf_op jit(solution)/shard_map/ppermute | solution.py:27
  13.8 11.4 %collective-permute-start.1 = (f32[3,8,16,128]{3,2,1,0:T(8,128)S(1)}, f32[3,8,16,128]{3,2,1,0:T(8,128)S(1)}, u32[]{:S(2)}, u32[]{:S(2)}) collective-permute-start(f32[3,8,16,128]{3,2,1,0:T(8,128)S(1)} %pad_maximum_fusion.4), channel_id=1, source_target_pairs={{64,0},{128,64},{192,128},{256,192},{320,256},{384,320},{448,384},... | collective-permute-start | bytes 589832 | tf_op jit(solution)/shard_map/ppermute | solution.py:30
  25.2 0.9 bitcast_subtract_fusion.1
  26.1 0.7 constant_dynamic-update-slice_fusion.11
  26.8 0.7 constant_dynamic-update-slice_fusion.10
  27.5 10.0 %collective-permute-done.1 = f32[3,8,16,128]{3,2,1,0:T(8,128)S(1)} collective-permute-done((f32[3,8,16,128]{3,2,1,0:T(8,128)S(1)}, f32[3,8,16,128]{3,2,1,0:T(8,128)S(1)}, u32[]{:S(2)}, u32[]{:S(2)}) %collective-permute-start.1) | collective-permute-done | bytes 196640 | tf_op jit(solution)/shard_map/ppermute | solution.py:30
  37.6 0.9 pad_maximum_fusion.1
  38.5 7.9 %collective-permute-start.2 = (f32[3,24,8,128]{3,2,1,0:T(8,128)S(1)}, f32[3,24,8,128]{3,2,1,0:T(8,128)S(1)}, u32[]{:S(2)}, u32[]{:S(2)}) collective-permute-start(f32[3,24,8,128]{3,2,1,0:T(8,128)S(1)} %get-tuple-element.34), channel_id=1, source_target_pairs={{0,1},{1,2},{2,3},{3,4},{4,5},{5,6},{6,7},{7,8},{8,9},{9,10},{10,1... | collective-permute-start | bytes 884744 | tf_op jit(solution)/shard_map/ppermute | solution.py:27
  46.4 1.9 %collective-permute-start.3 = (f32[3,24,8,128]{3,2,1,0:T(8,128)S(1)}, f32[3,24,8,128]{3,2,1,0:T(8,128)S(1)}, u32[]{:S(2)}, u32[]{:S(2)}) collective-permute-start(f32[3,24,8,128]{3,2,1,0:T(8,128)S(1)} %get-tuple-element.35), channel_id=1, source_target_pairs={{1,0},{2,1},{3,2},{4,3},{5,4},{6,5},{7,6},{8,7},{9,8},{10,9},{11,1... | collective-permute-start | bytes 884744 | tf_op jit(solution)/shard_map/ppermute | solution.py:30
  48.5 1.6 %collective-permute-done.2 = f32[3,24,8,128]{3,2,1,0:T(8,128)S(1)} collective-permute-done((f32[3,24,8,128]{3,2,1,0:T(8,128)S(1)}, f32[3,24,8,128]{3,2,1,0:T(8,128)S(1)}, u32[]{:S(2)}, u32[]{:S(2)}) %collective-permute-start.2) | collective-permute-done | bytes 294944 | tf_op jit(solution)/shard_map/ppermute | solution.py:27
  50.1 4.7 %collective-permute-done.3 = f32[3,24,8,128]{3,2,1,0:T(8,128)S(1)} collective-permute-done((f32[3,24,8,128]{3,2,1,0:T(8,128)S(1)}, f32[3,24,8,128]{3,2,1,0:T(8,128)S(1)}, u32[]{:S(2)}, u32[]{:S(2)}) %collective-permute-start.3) | collective-permute-done | bytes 294944 | tf_op jit(solution)/shard_map/ppermute | solution.py:30
  54.9 1.0 convolution_bitcast_fusion.3
  56.0 1.0 convolution_bitcast_fusion.2
  57.0 0.8 fusion.166
  57.8 0.8 fusion.167
  58.7 0.3 fusion.33
  59.5 1.0 convolution_bitcast_fusion.1
  60.5 1.0 convolution_bitcast_fusion
  61.5 0.8 fusion.168
  62.3 0.8 fusion.169
  63.2 0.3 fusion.30
  64.2 1.0 convolution_bitcast_fusion.4
  65.2 9.9 %all-to-all-start = ((f32[64,128,1]{1,2,0:T(1,128)}), f32[64,128,1]{1,2,0:T(1,128)S(1)}, u32[]{:S(2)}, u32[]{:S(2)}) async-start(f32[64,128,1]{1,2,0:T(1,128)} %convolution_bitcast_fusion.4), calls=%async_computation | async-start | bytes 65536 | tf_op jit(solution)/shard_map/all_to_all | solution.py:167
  75.4 9.3 %all-to-all-done = f32[64,128,1]{1,2,0:T(1,128)S(1)} async-done(((f32[64,128,1]{1,2,0:T(1,128)}), f32[64,128,1]{1,2,0:T(1,128)S(1)}, u32[]{:S(2)}, u32[]{:S(2)}) %all-to-all-start) | async-done | bytes 32800 | tf_op jit(solution)/shard_map/all_to_all | solution.py:167
  84.7 1.7 %fusion = f32[64,1,64]{2,1,0:T(1,128)S(1)} fusion(f32[64,128,1]{1,2,0:T(1,128)S(1)} %bitcast.513, s32[64,128]{1,0:T(8,128)S(1)} %get-tuple-element.49), kind=kOutput, calls=%fused_computation.2 | convolution fusion | flops 6815744 | bytes 81920 | tf_op jit(solution)/shard_map/psk,ps->pk/dot_general | solution.py:132
  86.6 7.5 %collective-permute-start.4 = (f32[12,8,128]{2,1,0:T(8,128)S(1)}, f32[12,8,128]{2,1,0:T(8,128)S(1)}, u32[]{:S(2)}, u32[]{:S(2)}) collective-permute-start(f32[12,8,128]{2,1,0:T(8,128)S(1)} %get-tuple-element.42), channel_id=1, source_target_pairs={{0,64},{64,128},{128,192},{192,256},{256,320},{320,384},{384,448},... | collective-permute-start | bytes 147464 | tf_op jit(solution)/shard_map/ppermute | solution.py:27
  94.1 5.2 %collective-permute-start.5 = (f32[12,8,128]{2,1,0:T(8,128)S(1)}, f32[12,8,128]{2,1,0:T(8,128)S(1)}, u32[]{:S(2)}, u32[]{:S(2)}) collective-permute-start(f32[12,8,128]{2,1,0:T(8,128)S(1)} %get-tuple-element.43), channel_id=1, source_target_pairs={{64,0},{128,64},{192,128},{256,192},{320,256},{384,320},{448,384},... | collective-permute-start | bytes 147464 | tf_op jit(solution)/shard_map/ppermute | solution.py:30
  99.4 7.3 %collective-permute-done.5 = f32[12,8,128]{2,1,0:T(8,128)S(1)} collective-permute-done((f32[12,8,128]{2,1,0:T(8,128)S(1)}, f32[12,8,128]{2,1,0:T(8,128)S(1)}, u32[]{:S(2)}, u32[]{:S(2)}) %collective-permute-start.5) | collective-permute-done | bytes 49184 | tf_op jit(solution)/shard_map/ppermute | solution.py:30
  106.9 2.7 %collective-permute-start.6 = (f32[12,48,8]{2,1,0:T(8,128)S(1)}, f32[12,48,8]{2,1,0:T(8,128)S(1)}, u32[]{:S(2)}, u32[]{:S(2)}) collective-permute-start(f32[12,48,8]{2,1,0:T(8,128)S(1)} %get-tuple-element.40), channel_id=1, source_target_pairs={{0,1},{1,2},{2,3},{3,4},{4,5},{5,6},{6,7},{7,8},{8,9},{9,10},{10,1... | collective-permute-start | bytes 55304 | tf_op jit(solution)/shard_map/ppermute | solution.py:27
  109.6 1.9 %collective-permute-start.7 = (f32[12,48,8]{2,1,0:T(8,128)S(1)}, f32[12,48,8]{2,1,0:T(8,128)S(1)}, u32[]{:S(2)}, u32[]{:S(2)}) collective-permute-start(f32[12,48,8]{2,1,0:T(8,128)S(1)} %get-tuple-element.41), channel_id=1, source_target_pairs={{1,0},{2,1},{3,2},{4,3},{5,4},{6,5},{7,6},{8,7},{9,8},{10,9},{11,1... | collective-permute-start | bytes 55304 | tf_op jit(solution)/shard_map/ppermute | solution.py:30
  111.5 1.7 %collective-permute-done.6 = f32[12,48,8]{2,1,0:T(8,128)S(1)} collective-permute-done((f32[12,48,8]{2,1,0:T(8,128)S(1)}, f32[12,48,8]{2,1,0:T(8,128)S(1)}, u32[]{:S(2)}, u32[]{:S(2)}) %collective-permute-start.6) | collective-permute-done | bytes 18464 | tf_op jit(solution)/shard_map/ppermute | solution.py:27
  113.2 4.7 %collective-permute-done.7 = f32[12,48,8]{2,1,0:T(8,128)S(1)} collective-permute-done((f32[12,48,8]{2,1,0:T(8,128)S(1)}, f32[12,48,8]{2,1,0:T(8,128)S(1)}, u32[]{:S(2)}, u32[]{:S(2)}) %collective-permute-start.7) | collective-permute-done | bytes 18464 | tf_op jit(solution)/shard_map/ppermute | solution.py:30
  117.9 0.3 pad_maximum_fusion.2
  118.2 0.3 fusion.78
  118.5 0.3 fusion.65
  118.8 0.3 fusion.52
  119.1 0.3 fusion.132
  119.4 0.3 fusion.119
  119.6 0.3 fusion.106
  120.2 0.7 fusion.146
  120.9 1.7 %fusion.2 = f32[64,128,1]{1,2,0:T(1,128)} fusion(f32[64,64,1]{1,2,0:T(1,128)S(1)} %bitcast.517, s32[64,128]{1,0:T(8,128)S(1)} %get-tuple-element.48), kind=kOutput, calls=%fused_computation.9 | convolution fusion | flops 6815744 | bytes 81920 | tf_op jit(solution)/shard_map/psk,pk->ps/dot_general | solution.py:124
  122.6 10.9 %all-to-all-start.1 = ((f32[64,128,1]{1,2,0:T(1,128)}), f32[64,128,1]{1,2,0:T(1,128)S(1)}, u32[]{:S(2)}, u32[]{:S(2)}) async-start(f32[64,128,1]{1,2,0:T(1,128)} %fusion.2), calls=%async_computation.1 | async-start | bytes 65536 | tf_op jit(solution)/shard_map/all_to_all | solution.py:187
  133.5 0.6 slice.885
  134.1 8.9 %all-to-all-done.1 = f32[64,128,1]{1,2,0:T(1,128)S(1)} async-done(((f32[64,128,1]{1,2,0:T(1,128)}), f32[64,128,1]{1,2,0:T(1,128)S(1)}, u32[]{:S(2)}, u32[]{:S(2)}) %all-to-all-start.1) | async-done | bytes 32800 | tf_op jit(solution)/shard_map/all_to_all | solution.py:187
  143.1 0.3 fusion.39
  143.5 0.7 reshape_reshape.7
  (69 shorter events, 2.6 us)
Async XLA Ops:
  2.3 25.3 %collective-permute-start = (f32[3,8,16,128]{3,2,1,0:T(8,128)S(1)}, f32[3,8,16,128]{3,2,1,0:T(8,128)S(1)}, u32[]{:S(2)}, u32[]{:S(2)}) collective-permute-start(f32[3,8,16,128]{3,2,1,0:T(8,128)S(1)} %pad_maximum_fusion.4), channel_id=1, source_target_pairs={{0,64},{64,128},{128,192},{192,256},{256,320},{320,384},{384,448},... | collective-permute-start | bytes 589832 | tf_op jit(solution)/shard_map/ppermute | solution.py:27
  13.8 23.8 %collective-permute-start.1 = (f32[3,8,16,128]{3,2,1,0:T(8,128)S(1)}, f32[3,8,16,128]{3,2,1,0:T(8,128)S(1)}, u32[]{:S(2)}, u32[]{:S(2)}) collective-permute-start(f32[3,8,16,128]{3,2,1,0:T(8,128)S(1)} %pad_maximum_fusion.4), channel_id=1, source_target_pairs={{64,0},{128,64},{192,128},{256,192},{320,256},{384,320},{448,384},... | collective-permute-start | bytes 589832 | tf_op jit(solution)/shard_map/ppermute | solution.py:30
  27.5 20.8 %copy-start.8 = (s32[1,64,128]{2,1,0:T(8,128)S(1)}, s32[1,64,128]{2,1,0:T(8,128)}, u32[]{:S(2)}) copy-start(s32[1,64,128]{2,1,0:T(8,128)} %param.25) | copy-start | bytes 98308
  27.5 20.9 %copy-start.9 = (s32[1,64,128]{2,1,0:T(8,128)S(1)}, s32[1,64,128]{2,1,0:T(8,128)}, u32[]{:S(2)}) copy-start(s32[1,64,128]{2,1,0:T(8,128)} %param.23) | copy-start | bytes 98308
  27.5 27.2 %copy-start = (f32[8,16,128]{2,1,0:T(8,128)S(1)}, f32[8,16,128]{2,1,0:T(8,128)}, u32[]{:S(2)}) copy-start(f32[8,16,128]{2,1,0:T(8,128)} %param.16) | copy-start | bytes 196612
  38.5 11.6 %collective-permute-start.2 = (f32[3,24,8,128]{3,2,1,0:T(8,128)S(1)}, f32[3,24,8,128]{3,2,1,0:T(8,128)S(1)}, u32[]{:S(2)}, u32[]{:S(2)}) collective-permute-start(f32[3,24,8,128]{3,2,1,0:T(8,128)S(1)} %get-tuple-element.34), channel_id=1, source_target_pairs={{0,1},{1,2},{2,3},{3,4},{4,5},{5,6},{6,7},{7,8},{8,9},{9,10},{10,1... | collective-permute-start | bytes 884744 | tf_op jit(solution)/shard_map/ppermute | solution.py:27
  46.4 8.3 %collective-permute-start.3 = (f32[3,24,8,128]{3,2,1,0:T(8,128)S(1)}, f32[3,24,8,128]{3,2,1,0:T(8,128)S(1)}, u32[]{:S(2)}, u32[]{:S(2)}) collective-permute-start(f32[3,24,8,128]{3,2,1,0:T(8,128)S(1)} %get-tuple-element.35), channel_id=1, source_target_pairs={{1,0},{2,1},{3,2},{4,3},{5,4},{6,5},{7,6},{8,7},{9,8},{10,9},{11,1... | collective-permute-start | bytes 884744 | tf_op jit(solution)/shard_map/ppermute | solution.py:30
  48.5 6.5 %copy-start.4 = (f32[4,4,1,1]{1,0,3,2:T(4,128)S(1)}, f32[4,4,1,1]{1,0,3,2:T(4,128)}, u32[]{:S(2)}) copy-start(f32[4,4,1,1]{1,0,3,2:T(4,128)} %constant.140) | copy-start | bytes 196
  54.9 1.1 copy-start.5
  63.8 11.4 %copy-start.1 = (f32[6,32,128]{2,1,0:T(8,128)S(1)}, f32[6,32,128]{2,1,0:T(8,128)}, u32[]{:S(2)}) copy-start(f32[6,32,128]{2,1,0:T(8,128)} %param.21) | copy-start | bytes 294916
  63.8 11.4 %copy-start.2 = (s32[6,32,128]{2,1,0:T(8,128)S(1)}, s32[6,32,128]{2,1,0:T(8,128)}, u32[]{:S(2)}) copy-start(s32[6,32,128]{2,1,0:T(8,128)} %param.20) | copy-start | bytes 294916
  63.8 20.9 %copy-start.6 = (f32[1,64,128]{2,1,0:T(8,128)S(1)}, f32[1,64,128]{2,1,0:T(8,128)}, u32[]{:S(2)}) copy-start(f32[1,64,128]{2,1,0:T(8,128)} %param.24) | copy-start | bytes 98308
  65.2 19.4 %all-to-all-start = ((f32[64,128,1]{1,2,0:T(1,128)}), f32[64,128,1]{1,2,0:T(1,128)S(1)}, u32[]{:S(2)}, u32[]{:S(2)}) async-start(f32[64,128,1]{1,2,0:T(1,128)} %convolution_bitcast_fusion.4), calls=%async_computation | async-start | bytes 65536 | tf_op jit(solution)/shard_map/all_to_all | solution.py:167
  86.6 12.7 %collective-permute-start.4 = (f32[12,8,128]{2,1,0:T(8,128)S(1)}, f32[12,8,128]{2,1,0:T(8,128)S(1)}, u32[]{:S(2)}, u32[]{:S(2)}) collective-permute-start(f32[12,8,128]{2,1,0:T(8,128)S(1)} %get-tuple-element.42), channel_id=1, source_target_pairs={{0,64},{64,128},{128,192},{192,256},{256,320},{320,384},{384,448},... | collective-permute-start | bytes 147464 | tf_op jit(solution)/shard_map/ppermute | solution.py:27
  94.1 12.5 %collective-permute-start.5 = (f32[12,8,128]{2,1,0:T(8,128)S(1)}, f32[12,8,128]{2,1,0:T(8,128)S(1)}, u32[]{:S(2)}, u32[]{:S(2)}) collective-permute-start(f32[12,8,128]{2,1,0:T(8,128)S(1)} %get-tuple-element.43), channel_id=1, source_target_pairs={{64,0},{128,64},{192,128},{256,192},{320,256},{384,320},{448,384},... | collective-permute-start | bytes 147464 | tf_op jit(solution)/shard_map/ppermute | solution.py:30
  106.9 6.4 %collective-permute-start.6 = (f32[12,48,8]{2,1,0:T(8,128)S(1)}, f32[12,48,8]{2,1,0:T(8,128)S(1)}, u32[]{:S(2)}, u32[]{:S(2)}) collective-permute-start(f32[12,48,8]{2,1,0:T(8,128)S(1)} %get-tuple-element.40), channel_id=1, source_target_pairs={{0,1},{1,2},{2,3},{3,4},{4,5},{5,6},{6,7},{7,8},{8,9},{9,10},{10,1... | collective-permute-start | bytes 55304 | tf_op jit(solution)/shard_map/ppermute | solution.py:27
  109.6 8.3 %collective-permute-start.7 = (f32[12,48,8]{2,1,0:T(8,128)S(1)}, f32[12,48,8]{2,1,0:T(8,128)S(1)}, u32[]{:S(2)}, u32[]{:S(2)}) collective-permute-start(f32[12,48,8]{2,1,0:T(8,128)S(1)} %get-tuple-element.41), channel_id=1, source_target_pairs={{1,0},{2,1},{3,2},{4,3},{5,4},{6,5},{7,6},{8,7},{9,8},{10,9},{11,1... | collective-permute-start | bytes 55304 | tf_op jit(solution)/shard_map/ppermute | solution.py:30
  119.9 23.2 %copy-start.7 = (f32[1,64,128]{2,1,0:T(8,128)S(1)}, f32[1,64,128]{2,1,0:T(8,128)}, u32[]{:S(2)}) copy-start(f32[1,64,128]{2,1,0:T(8,128)} %param.27) | copy-start | bytes 98308
  120.8 23.3 %copy-start.3 = (f32[32,128]{1,0:T(8,128)}, f32[32,128]{1,0:T(8,128)S(1)}, u32[]{:S(2)}) copy-start(f32[32,128]{1,0:T(8,128)S(1)} %get-tuple-element.14) | copy-start | bytes 49156
  122.6 20.5 %all-to-all-start.1 = ((f32[64,128,1]{1,2,0:T(1,128)}), f32[64,128,1]{1,2,0:T(1,128)S(1)}, u32[]{:S(2)}, u32[]{:S(2)}) async-start(f32[64,128,1]{1,2,0:T(1,128)} %fusion.2), calls=%async_computation.1 | async-start | bytes 65536 | tf_op jit(solution)/shard_map/all_to_all | solution.py:187
where the time goes:
time: 145 us; the launch traced here: 144 us
  starting transfers between devices  70.9 us (49%)
  waiting for transfers between devices  48.3 us (33%)
  matrix products  11.9 us (8%)
  other arithmetic  8.24 us (6%)
  local copies, waits for them, and re-layouts  3.61 us (2%)
    ppermute x4, starting transfers between devices, with_halo(): lax.ppermute(lax.slice_in_dim(block, block.shape[dim] - width, None, axis...  29.6 us
    ppermute x4, waiting for transfers between devices, with_halo(): lax.ppermute(lax.slice_in_dim(block, 0, width, axis=dim), axis, backward)  26.7 us
    all_to_all x2, starting transfers between devices, on_device(): lax.all_to_all(outgoing, 'tile', split_axis=0, concat_axis=0, tiled=True)  20.8 us
    ppermute x4, starting transfers between devices, with_halo(): lax.ppermute(lax.slice_in_dim(block, 0, width, axis=dim), axis, backward)  20.4 us
    all_to_all x2, waiting for transfers between devices, on_device(): lax.all_to_all(outgoing, 'tile', split_axis=0, concat_axis=0, tiled=True)  18.2 us
    dot_general x4, matrix products, along_first(): jnp.einsum('ik,ekyl->eiyl', matrix, shaped, precision=lax.Precision.HIGHEST)  4.06 us
    ppermute x4, waiting for transfers between devices, with_halo(): lax.ppermute(lax.slice_in_dim(block, block.shape[dim] - width, None, axis...  3.33 us
    dot_general x4, matrix products, along_second(): jnp.einsum('ik,xekl->xeil', matrix, shaped, precision=lax.Precision.HIGHEST)  3.15 us
  transfers between devices with their start and end apart: 10, of which 8 were waited for; matrix products, arithmetic and copies ran while one was open for 2% of the time, Pallas kernels for 0%

commit v1 on v0

v1 whole, which is shorter than its diff:
```python
import jax
import jax.numpy as jnp
import numpy as np
from jax import lax
from jax.experimental import pallas as pl
from jax.experimental.pallas import tpu as pltpu
from jax.sharding import PartitionSpec as P

F32 = jnp.float32
MESH = pl.DeviceIdType.MESH
HIGHEST = lax.Precision.HIGHEST
NT = (((1,), (1,)), ((), ()))
NN = (((1,), (0,)), ((), ()))

SUBSTEPS = 2
SUBCYCLES = 8
NC = 16
NR = 64
AX, AY = 8, 16
PTS = AX * AY
OX, OY = 32, 128
ROWS = OX + 16

atmos_step = 0.05
viscosity = 0.05
ocean_step = 0.2
wave_speed = 1.0
friction = 0.05

HALO, TABLE, EDGE, OCEAN, MATRIX, GATHER, UP, FAR = 0, 1, 2, 4, 7, 10, 11, 12


def gll_derivative():
    points = np.array([-1.0, -1.0 / np.sqrt(5.0), 1.0 / np.sqrt(5.0), 1.0])
    weights = np.array(
        [1.0 / np.prod([points[j] - points[k] for k in range(4) if k != j]) for j in range(4)]
    )
    matrix = np.zeros((4, 4))
    for i in range(4):
        for j in range(4):
            if i != j:
                matrix[i, j] = weights[j] / weights[i] / (points[i] - points[j])
        matrix[i, i] = -np.sum(matrix[i])
    return matrix


def point_operators():
    first = gll_derivative()
    second = first @ first
    along_x = lambda m: np.kron(np.kron(np.eye(AX // 4), m), np.eye(AY))
    along_y = lambda m: np.kron(np.eye(AX), np.kron(np.eye(AY // 4), m))
    curvature = viscosity * (along_x(second) + along_y(second))
    return np.concatenate([curvature, along_x(first), along_y(first)]).astype(np.float32)


def iota(shape, dim):
    return lax.broadcasted_iota(jnp.int32, shape, dim)


def roll(x, shift, axis):
    return pltpu.roll(x, shift % x.shape[axis], axis)


def kernel(
    atmos_in, wind_in, height_in, potential_in, neigh_in, coup_in,
    dsrc_in, dtgt_in, dwgt_in, usrc_in, utgt_in, uwgt_in, oper_in,
    atmos_out, height_out, potential_out, flux_out,
    atmos_v, wind_v, neigh_v, coup_v, dsrc_v, dtgt_v, dwgt_v, usrc_v, utgt_v, uwgt_v, oper_v,
    surf_h, tab_s, tab_r, edge_s, edge_r, oc0, oc_pack, oc_right, oc_left,
    mx0, mx_pack, mx_right, mx_left, g_s, g_r, h_s, u_r, part_v, wst_v,
    aout_v, pout_v, fout_v, in_sem, out_sem, ssem, rsem,
):
    c = lax.axis_index("comp")
    t = lax.axis_index("tile")
    k = t % 2
    r = t // 2
    z = t // 16
    y = (t // 2) % 8
    up_row = (c + 1) % NC
    down_row = (c + NC - 1) % NC
    right = (t + 1) % NR
    left = (t + NR - 1) % NR
    own_q = k * 32 + r

    def at(dc, dt):
        row = c if dc == 0 else (up_row if dc > 0 else down_row)
        col = t if dt == 0 else (right if dt > 0 else left)
        return (row, col)

    around = [(i, j) for i in (-1, 0, 1) for j in (-1, 0, 1) if (i, j) != (0, 0)]

    def send(src, dst, which, to, left_by=None):
        pltpu.make_async_remote_copy(
            src_ref=src, dst_ref=dst,
            send_sem=ssem.at[which if left_by is None else left_by], recv_sem=rsem.at[which],
            device_id=to, device_id_type=MESH,
        ).start()

    def take(ref, sem):
        pltpu.make_async_copy(ref, ref, sem).wait()

    loads = [
        pltpu.make_async_copy(src, dst, in_sem.at[i])
        for i, (src, dst) in enumerate([
            (atmos_in, atmos_v), (oper_in, oper_v), (wind_in, wind_v),
            (dsrc_in, dsrc_v), (usrc_in, usrc_v),
            (neigh_in, neigh_v), (coup_in, coup_v),
            (height_in, oc0.at[0, pl.ds(0, OX)]), (potential_in, oc0.at[1, pl.ds(0, OX)]),
            (dtgt_in, dtgt_v), (dwgt_in, dwgt_v), (utgt_in, utgt_v), (uwgt_in, uwgt_v),
        ])
    ]
    for load in loads:
        load.start()
    surf_h[:, 9:16, :] = jnp.zeros((3, 7, PTS), F32)

    barrier = pltpu.get_barrier_semaphore()

    def greet(to):
        pl.semaphore_signal(barrier, inc=1, device_id=to, device_id_type=MESH)

    for i, j in around:
        if i != 0:
            greet(at(i, j))

    def greet_far(i, carry):
        greet((up_row, i))
        greet((down_row, 48 + i))
        return carry

    lax.fori_loop(0, 16, greet_far, 0)

    def greet_row(i, carry):
        greet((c, (t + 1 + i) % NR))
        return carry

    lax.fori_loop(0, NR - 1, greet_row, 0)

    lane8 = iota((8, 128), 1)
    last = jnp.where(lane8 == 127, 1.0, 0.0).astype(F32)
    pick_last = lambda block: lax.dot_general(
        last, block, NT, precision=HIGHEST, preferred_element_type=F32
    )[0:1]
    loads[0].wait()
    loads[1].wait()
    loads[2].wait()
    atmos = atmos_v[...]
    east = wind_v[0:PTS].astype(F32)
    north = wind_v[PTS:2 * PTS].astype(F32)
    surf_h[0, 4:5] = pick_last(atmos)
    surf_h[1, 4:5] = pick_last(east)
    surf_h[2, 4:5] = pick_last(north)

    def rate_of(a):
        res = lax.dot_general(oper_v[...], a, NN, precision=HIGHEST, preferred_element_type=F32)
        return res[0:PTS] - (east * res[PTS:2 * PTS] + north * res[2 * PTS:3 * PTS])

    def stage_edges(step, rate):
        edge_s[step, 0:16] = rate[0:16]
        edge_s[step, 16:32] = rate[112:128]
        shaped = rate.reshape(AX, AY, 128)
        edge_s[step, 32:40] = shaped[:, 0]
        edge_s[step, 40:48] = shaped[:, 15]

    def send_edges(step):
        s = lambda lo, n: edge_s.at[step, pl.ds(lo, n)]
        d = lambda lo, n: edge_r.at[step, pl.ds(lo, n)]
        which = EDGE + step
        send(s(0, 16), d(0, 16), which, at(-1, 0))
        send(s(16, 16), d(16, 16), which, at(1, 0))
        send(s(0, 1), d(48, 1), which, at(-1, -1))
        send(s(15, 1), d(49, 1), which, at(-1, 1))
        send(s(16, 1), d(50, 1), which, at(1, -1))
        send(s(31, 1), d(51, 1), which, at(1, 1))
        send(s(32, 8), d(32, 8), which, at(0, -1))
        send(s(40, 8), d(40, 8), which, at(0, 1))

    rate0 = rate_of(atmos)
    stage_edges(0, rate0)

    loads[3].wait()
    loads[4].wait()
    band = iota((NR, 128), 0)
    tab_s[0] = (dsrc_v[...] - 2 * band).astype(F32)
    tab_s[1] = (usrc_v[...] - 64 * band).astype(F32)
    for d in range(2):
        tab_r[d, pl.ds(own_q, 1)] = tab_s[d, pl.ds(t, 1)]

    for i in (5, 6, 7, 8):
        loads[i].wait()
    base = iota((OX, OY), 0) * (OY + 2) + iota((OX, OY), 1)
    links = [(neigh_v[l] - base, coup_v[l]) for l in range(6)]

    def weight_of(di, dj):
        code = (di + 1) * (OY + 2) + dj + 1
        total = jnp.zeros((OX, OY), F32)
        for place, coef in links:
            total = total + jnp.where(place == code, coef, 0.0)
        return total

    own = slice(0, OX)
    oc0[2, own] = weight_of(-1, 0)
    oc0[3, own] = weight_of(1, 0)
    oc0[4, own] = weight_of(0, -1)
    oc0[5, own] = weight_of(0, 1)
    oc0[6, own] = weight_of(1, 1) - weight_of(1, -1)
    oc0[7, own] = weight_of(-1, -1) - weight_of(-1, 1)

    lane_o = iota((OX, OY), 1)

    def pack(fields):
        packed = jnp.zeros((OX, OY), F32)
        for f, value in enumerate(fields):
            packed = jnp.where(lane_o // 8 == f, roll(value, 8 * f, 1), packed)
            packed = jnp.where(lane_o // 8 == 8 + f, roll(value, 72 + 8 * f, 1), packed)
        return packed

    def send_block(full, packed, rt, lf, which):
        top, bottom = pl.ds(0, 8), pl.ds(24, 8)
        send(full.at[:, bottom], full.at[:, pl.ds(40, 8)], which, at(1, 0))
        send(full.at[:, top], full.at[:, pl.ds(32, 8)], which, at(-1, 0))
        send(packed.at[bottom], rt.at[pl.ds(40, 8)], which + 1, at(1, -1))
        send(packed.at[top], rt.at[pl.ds(32, 8)], which + 1, at(-1, -1))
        send(packed, rt.at[pl.ds(0, OX)], which + 1, at(0, -1))
        send(packed.at[bottom], lf.at[pl.ds(40, 8)], which + 2, at(1, 1))
        send(packed.at[top], lf.at[pl.ds(32, 8)], which + 2, at(-1, 1))
        send(packed, lf.at[pl.ds(0, OX)], which + 2, at(0, 1))

    def take_block(full, rt, lf, sems, which):
        take(full.at[:, pl.ds(32, 16)], sems.at[which])
        take(rt, sems.at[which + 1])
        take(lf, sems.at[which + 2])

    lane_x = iota((ROWS, OY), 1)

    def beside(rt, lf, f):
        from_right = roll(rt, -8 * f, 1)
        from_left = roll(lf, 56 - 8 * f, 1)
        return jnp.where(lane_x < 8, from_right, jnp.where(lane_x >= 120, from_left, 0.0))

    oc_pack[...] = pack([oc0[f, own] for f in range(8)])

    far = jnp.where((z == 0) | (z == 3), 1, 0)
    pl.semaphore_wait(barrier, NR - 1 + 6 + NR * far)

    centre = pl.ds(4, 1)
    for i, j in around:
        send(surf_h.at[:, centre], surf_h.at[:, pl.ds(4 - 3 * i - j, 1)], HALO, at(i, j))

    def ordered(i):
        j = i // 8
        step_y = 4 + ((j + 1) // 2) * (2 * (j % 2) - 1)
        zk = (i + 1) % 8
        return ((z + zk // 2) % 4) * 16 + ((y + step_y) % 8) * 2 + (k + zk) % 2

    def send_table(i, carry):
        to = ordered(i)
        send(tab_s.at[:, pl.ds(to, 1)], tab_r.at[:, pl.ds(own_q, 1)], TABLE, (c, to))
        return carry

    lax.fori_loop(0, NR - 1, send_table, 0)
    send_edges(0)
    send_block(oc0, oc_pack, oc_right, oc_left, OCEAN)

    lane_s = iota((16, PTS), 1)
    xs, ys = lane_s // AY, lane_s % AY

    def pairs(values, after, before, pos):
        return jnp.where(
            pos == 3, 0.5 * (values + after), jnp.where(pos == 0, 0.5 * (values + before), values)
        )

    take(edge_r.at[0, pl.ds(0, 24)], rsem.at[HALO])
    surf = surf_h[0]
    surf_e = surf_h[1]
    surf_n = surf_h[2]
    for _ in range(SUBSTEPS):
        res = lax.dot_general(surf, oper_v[...], NT, precision=HIGHEST, preferred_element_type=F32)
        rate = res[:, 0:PTS] - (surf_e * res[:, PTS:2 * PTS] + surf_n * res[:, 2 * PTS:3 * PTS])
        nxt, prv = roll(rate, -16, 1), roll(rate, 16, 1)
        after = jnp.where(xs == AX - 1, roll(nxt, -3, 0), nxt)
        before = jnp.where(xs == 0, roll(prv, 3, 0), prv)
        rate = pairs(rate, after, before, xs % 4)
        after = jnp.where(ys == AY - 1, roll(roll(rate, 15, 1), -1, 0), roll(rate, -1, 1))
        before = jnp.where(ys == 0, roll(roll(rate, -15, 1), 1, 0), roll(rate, 1, 1))
        surf = surf + atmos_step * pairs(rate, after, before, ys % 4)
    surf_row = surf[4:5]
    g_s[0:1] = surf_row
    g_r[pl.ds(k * ROWS + r, 1)] = surf_row

    @pl.when(far == 1)
    def _():
        row = jnp.where(z == 0, down_row, up_row)
        place = k * ROWS + jnp.where(z == 0, 32, 40) + y

        def send_far(i, carry):
            send(g_s.at[pl.ds(0, 1)], g_r.at[pl.ds(place, 1)], GATHER, (row, ordered(i)), FAR)
            return carry

        lax.fori_loop(0, NR, send_far, 0)

    def send_surface(i, carry):
        send(g_s.at[pl.ds(0, 1)], g_r.at[pl.ds(k * ROWS + r, 1)], GATHER, (c, ordered(i)))
        return carry

    lax.fori_loop(0, NR - 1, send_surface, 0)

    row_q = iota((NR, 128), 0)
    peer_q = 2 * (row_q % 32) + row_q // 32
    lane_64 = iota((NR, 128), 1)

    def by_core(ref):
        return jnp.concatenate(
            [ref[pl.ds(0, 32, stride=2), :], ref[pl.ds(1, 32, stride=2), :]], axis=0
        )

    def turned(value):
        tall = jnp.concatenate([value, jnp.zeros((128 - NR, 128), F32)], axis=0).T
        return jnp.where(lane_64 < 64, tall[0:64], roll(tall[64:128], 64, 1))

    def matrices(cell, second, weight):
        cell_t = turned(cell)
        one = weight * second
        one_t = turned(one)
        zero_t = turned(weight - one)

        def group(g, carry):
            for i in range(8):
                n = g * 8 + i
                hit = cell_t == n.astype(F32)
                part_v[0, pl.ds(n, 1)] = jnp.sum(jnp.where(hit, zero_t, 0.0), axis=0, keepdims=True)
                part_v[1, pl.ds(n, 1)] = jnp.sum(jnp.where(hit, one_t, 0.0), axis=0, keepdims=True)
            return carry

        lax.fori_loop(0, 8, group, 0)
        return [part_v[j] + roll(part_v[j], 64, 1) for j in range(2)]

    for i in (9, 10):
        loads[i].wait()
    take(tab_r.at[:, pl.ds(0, NR - 1)], rsem.at[TABLE])
    down = matrices(
        (by_core(dtgt_v) - 64 * peer_q).astype(F32), tab_r[0], by_core(dwgt_v)
    )
    for j in range(2):
        cells = jnp.concatenate([down[j], roll(down[j], -32, 1)], axis=0).T
        mx0[j, own] = cells[0:OX]
    mx_pack[...] = pack([mx0[j, own] for j in range(2)])
    send_block(mx0, mx_pack, mx_right, mx_left, MATRIX)

    row_a = iota((PTS, 128), 0)
    xa, ya = row_a // AY, row_a % AY
    row_e = iota((AX, 128), 0)

    def finish(step, a, rate):
        take(edge_r.at[step, pl.ds(0, 52)], rsem.at[EDGE + step])
        recv = lambda lo, n: edge_r[step, lo:lo + n]
        after = jnp.concatenate([rate[16:128], recv(0, 16)], axis=0)
        before = jnp.concatenate([recv(16, 16), rate[0:112]], axis=0)
        across = pairs(rate, after, before, xa % 4)

        def column(lo, beyond, ahead):
            col = recv(lo, 8)
            nxt = jnp.where(row_e == 7, beyond, roll(col, -1, 0))
            prv = jnp.where(row_e == 0, ahead, roll(col, 1, 0))
            col = pairs(col, nxt, prv, row_e % 4)
            return jnp.broadcast_to(col[:, None, :], (AX, AY, 128)).reshape(PTS, 128)

        east_col = column(32, recv(48, 1), recv(50, 1))
        west_col = column(40, recv(49, 1), recv(51, 1))
        after = jnp.where(ya == AY - 1, east_col, roll(across, -1, 0))
        before = jnp.where(ya == 0, west_col, roll(across, 1, 0))
        return a + atmos_step * pairs(across, after, before, ya % 4)

    atmos = finish(0, atmos, rate0)
    rate1 = rate_of(atmos)
    stage_edges(1, rate1)
    send_edges(1)

    for i in (11, 12):
        loads[i].wait()
    upward = matrices(
        tab_r[1], (by_core(utgt_v) - 2 * peer_q).astype(F32), by_core(uwgt_v)
    )
    up_cells = []
    blank = jnp.zeros((NR, 128), F32)
    for j in range(2):
        low = jnp.where(k == 0, upward[j], blank)
        high = jnp.where(k == 0, blank, upward[j])
        up_cells.append(jnp.concatenate([low, high], axis=0).T[0:NR])

    take_block(oc0, oc_right, oc_left, rsem, OCEAN)
    oc_rt, oc_lf = oc_right[...], oc_left[...]
    wide = [jnp.concatenate([oc0[f], beside(oc_rt, oc_lf, f)], axis=1) for f in range(8)]
    height, potential, w_n, w_s, w_w, w_e, pair_s, pair_n = wide
    w_se, w_sw = jnp.maximum(pair_s, 0.0), jnp.maximum(-pair_s, 0.0)
    w_nw, w_ne = jnp.maximum(pair_n, 0.0), jnp.maximum(-pair_n, 0.0)
    w_c = -(w_n + w_s + w_w + w_e + w_se + w_sw + w_nw + w_ne)
    for i, (value, shift) in enumerate([
        (w_nw, -1), (w_w, -1), (w_sw, -1),
        (w_n, 0), (w_c, 0), (w_s, 0),
        (w_ne, 1), (w_e, 1), (w_se, 1),
    ]):
        value = ocean_step * value
        wst_v[i] = value if shift == 0 else roll(value, shift, 1)

    atmos = finish(1, atmos, rate1)
    aout_v[...] = atmos
    atmos_copy = pltpu.make_async_copy(aout_v, atmos_out, out_sem.at[0])
    atmos_copy.start()

    take_block(mx0, mx_right, mx_left, rsem, MATRIX)
    mx_rt, mx_lf = mx_right[...], mx_left[...]
    mx1 = [beside(mx_rt, mx_lf, j) for j in range(2)]
    take(g_r.at[pl.ds(0, 95)], rsem.at[GATHER])
    even, odd = g_r[0:ROWS], g_r[ROWS:2 * ROWS]

    def column_of(block, point):
        return jnp.sum(jnp.where(lane_x == point, block, 0.0), axis=1, keepdims=True)

    near = jnp.zeros((ROWS, OY), F32)
    side = jnp.zeros((ROWS, OY), F32)
    for j in range(2):
        here = jnp.where(lane_x < 64, column_of(even, 2 * t + j), column_of(odd, 2 * t + j))
        there = jnp.where(
            lane_x < 64, column_of(even, 2 * right + j), column_of(odd, 2 * left + j)
        )
        near = near + mx0[j] * here
        side = side + mx1[j] * there
    forcing = ocean_step * jnp.concatenate([near, side], axis=1)

    for _ in range(SUBCYCLES):
        potential = (1.0 - friction) * potential + (ocean_step * wave_speed) * height + forcing
        above = roll(potential, 1, 0)
        below = roll(potential, -1, 0)
        sums = [
            wst_v[3 * j] * above + wst_v[3 * j + 1] * potential + wst_v[3 * j + 2] * below
            for j in range(3)
        ]
        height = height + sums[1] + roll(sums[0], 1, 1) + roll(sums[2], -1, 1)

    h_s[...] = height[0:OX, 0:OY]
    u_r[pl.ds(own_q, 1)] = h_s[pl.ds(r, 1)]

    def send_height(i, carry):
        to = ordered(i)
        send(h_s.at[pl.ds(to // 2, 1)], u_r.at[pl.ds(own_q, 1)], UP, (c, to))
        return carry

    lax.fori_loop(0, NR - 1, send_height, 0)
    pout_v[...] = potential[0:OX, 0:OY]
    height_copy = pltpu.make_async_copy(h_s, height_out, out_sem.at[1])
    potential_copy = pltpu.make_async_copy(pout_v, potential_out, out_sem.at[2])
    height_copy.start()
    potential_copy.start()

    take(edge_r.at[0, pl.ds(0, 24)], ssem.at[HALO])
    take(tab_r.at[:, pl.ds(0, NR - 1)], ssem.at[TABLE])
    take(edge_r.at[0, pl.ds(0, 52)], ssem.at[EDGE])
    take(edge_r.at[1, pl.ds(0, 52)], ssem.at[EDGE + 1])
    take_block(oc0, oc_right, oc_left, ssem, OCEAN)
    take_block(mx0, mx_right, mx_left, ssem, MATRIX)
    take(g_r.at[pl.ds(0, NR - 1)], ssem.at[GATHER])

    @pl.when(far == 1)
    def _():
        take(g_r.at[pl.ds(0, NR)], ssem.at[FAR])

    q_row = iota((AX, NR), 1)
    pick = jnp.where((q_row % 32) // 4 == iota((AX, NR), 0), 1.0, 0.0).astype(F32)
    column0 = 4 * (row_q % 4) + 2 * (row_q // 32)
    take(u_r.at[pl.ds(0, NR - 1)], rsem.at[UP])
    cells = u_r[...]
    spread = jnp.zeros((NR, 128), F32)
    for j in range(2):
        total = jnp.sum(up_cells[j] * cells, axis=1, keepdims=True)
        spread = spread + jnp.where(lane_64 == column0 + j, total, 0.0)
    flux = lax.dot_general(pick, spread, NN, precision=HIGHEST, preferred_element_type=F32)
    fout_v[...] = flux[:, 0:AY]
    flux_copy = pltpu.make_async_copy(fout_v, flux_out, out_sem.at[3])
    flux_copy.start()
    take(u_r.at[pl.ds(0, NR - 1)], ssem.at[UP])
    for copy in (atmos_copy, height_copy, potential_copy, flux_copy):
        copy.wait()


def on_device(
    atmos_state, wind_field, ocean_height, ocean_potential, ocean_neighbors, ocean_coupling,
    downward_source, downward_target, downward_weight,
    upward_source, upward_target, upward_weight,
):
    table = lambda value: value.reshape(NR, 128)
    any_spec = pl.BlockSpec(memory_space=pl.ANY)
    vm = lambda *shape, dtype=F32: pltpu.VMEM(shape, dtype)
    i32 = jnp.int32
    outs = pl.pallas_call(
        kernel,
        out_shape=[
            jax.ShapeDtypeStruct((PTS, 128), F32),
            jax.ShapeDtypeStruct((OX, OY), F32),
            jax.ShapeDtypeStruct((OX, OY), F32),
            jax.ShapeDtypeStruct((AX, AY), F32),
        ],
        in_specs=[any_spec] * 13,
        out_specs=[any_spec] * 4,
        scratch_shapes=[
            vm(PTS, 128), vm(2 * PTS, 128, dtype=jnp.bfloat16),
            vm(6, OX, OY, dtype=i32), vm(6, OX, OY),
            vm(NR, 128, dtype=i32), vm(NR, 128, dtype=i32), vm(NR, 128),
            vm(NR, 128, dtype=i32), vm(NR, 128, dtype=i32), vm(NR, 128),
            vm(3 * PTS, PTS),
            vm(3, 16, PTS), vm(2, NR, 128), vm(2, NR, 128), vm(2, 48, 128), vm(2, 56, 128),
            vm(8, ROWS, OY), vm(OX, OY), vm(ROWS, OY), vm(ROWS, OY),
            vm(2, ROWS, OY), vm(OX, OY), vm(ROWS, OY), vm(ROWS, OY),
            vm(8, 128), vm(2 * ROWS, 128), vm(OX, OY), vm(NR, 128),
            vm(2, NR, 128), vm(9, ROWS, 256),
            vm(PTS, 128), vm(OX, OY), vm(AX, AY),
            pltpu.SemaphoreType.DMA((13,)), pltpu.SemaphoreType.DMA((4,)),
            pltpu.SemaphoreType.DMA((13,)), pltpu.SemaphoreType.DMA((12,)),
        ],
        compiler_params=pltpu.CompilerParams(
            collective_id=0, has_side_effects=True, vmem_limit_bytes=60 * 1024 * 1024
        ),
        name="coupled_step",
    )(
        atmos_state.reshape(PTS, 128), wind_field.reshape(2 * PTS, 128),
        ocean_height, ocean_potential, ocean_neighbors, ocean_coupling,
        table(downward_source), table(downward_target), table(downward_weight),
        table(upward_source), table(upward_target), table(upward_weight),
        jnp.asarray(point_operators()),
    )
    return (outs[0].reshape(AX, AY, 128), outs[1], outs[2], outs[3])


def solution(mesh):
    cells = P(None, "comp", "tile")
    tables = P("comp", "tile", None)
    flat = P("comp", "tile")
    return jax.shard_map(
        on_device,
        mesh=mesh,
        in_specs=(tables, P(None, "comp", "tile", None), flat, flat, cells, cells) + (tables,) * 6,
        out_specs=(tables, flat, flat, flat),
        check_vma=False,
    )
```

time: 145 us -> 59 us (0.41)
  starting transfers between devices: 70.9 us -> 0 us
  Pallas kernels: 0 us -> 54.6 us
  waiting for transfers between devices: 48.3 us -> 0 us
  matrix products: 11.9 us -> 0 us
  other arithmetic: 8.24 us -> 0 us
    pallas_call x0 -> x1, Pallas kernels: none -> 54.6 us  [on_device(): pl.pallas_call(kernel, out_shape=[jax.ShapeDtypeStruct((PTS, 128), F32),...]
    ppermute x8 -> x0, starting transfers between devices: 50 us -> none  [the longest x4 29.6 us: with_halo(): lax.ppermute(lax.slice_in_dim(block, block.shape[dim] - width, None, axis...]
    ppermute x8 -> x0, waiting for transfers between devices: 30.1 us -> none  [the longest x4 26.7 us: with_halo(): lax.ppermute(lax.slice_in_dim(block, 0, width, axis=dim), axis, backward)]
    all_to_all x2 -> x0, starting transfers between devices: 20.8 us -> none  [on_device(): lax.all_to_all(outgoing, 'tile', split_axis=0, concat_axis=0, tiled=True)]
    all_to_all x2 -> x0, waiting for transfers between devices: 18.2 us -> none  [on_device(): lax.all_to_all(outgoing, 'tile', split_axis=0, concat_axis=0, tiled=True)]
    dot_general x12 -> x0, matrix products: 11.9 us -> none  [the longest x4 4.06 us: along_first(): jnp.einsum('ik,ekyl->eiyl', matrix, shaped, precision=lax.Precision.HIGHEST)]
    add x11 -> x0, other arithmetic: 2.98 us -> none  [the longest x8 1.9 us: on_device(): (1.0 - friction) * potential + ocean_step * (wave_speed * height + forcing)]
    unnamed x30 -> x10, local copies, waits for them, and re-layouts: 1.53 us -> 3.47 us
  transfers between devices with their start and end apart: 10 -> 0, of which waited for: 8 -> 0; matrix products, arithmetic and copies ran while one was open for 2% -> 0% of each run, Pallas kernels for 0% -> 0%
where the time goes in v1:
time: 59 us; the launch traced here: 58.8 us
  Pallas kernels  54.6 us (93%)
  local copies, waits for them, and re-layouts  3.47 us (6%)
  between operations  0.66 us (1%)
    pallas_call x1, Pallas kernels, on_device(): pl.pallas_call(kernel, out_shape=[jax.ShapeDtypeStruct((PTS, 128), F32),...  54.6 us
    unnamed x10, local copies, waits for them, and re-layouts  3.47 us

profile of v1, /device:TPU:1, one launch (start us, length us, event | category | flops | bytes accessed | tf_op | source)
XLA Modules:
  0.0 58.8 jit_solution(15068548033314448994)
XLA Ops:
  0.6 54.6 %coupled_step.1 = (f32[128,128]{1,0:T(8,128)}, f32[32,128]{1,0:T(8,128)}, f32[32,128]{1,0:T(8,128)}, f32[8,16]{1,0:T(8,128)}) custom-call(f32[128,128]{1,0:T(8,128)} %bitcast.9, bf16[256,128]{1,0:T(8,128)(2,1)} %bitcast.10, f32[32,128]{1,0:T(8,128)} %height_in.1, f32[32,128]{1,0:T(8,128)} %potential_in.1, s32[6,32,128]{2,1,0:T(8,128)} %neigh_in.1, ...), custom_call_target="tpu_custom_call" | custom-call | tf_op jit(solution)/shard_map/coupled_step/pallas_call | solution.py:494
  55.3 0.0 copy-start.1
  55.3 1.5 %copy.21 = f32[8,16,128]{2,1,0:T(8,128)} copy(f32[8,16,128]{2,1,0:T(8,128)} %bitcast.11) | data formatting | bytes 131072
  56.8 0.0 copy-done.1
  56.8 0.0 copy-start
  56.8 0.6 %copy.22 = f32[32,128]{1,0:T(8,128)} copy(f32[32,128]{1,0:T(8,128)S(1)} %copy-done.1) | data formatting | bytes 32768
  57.4 0.1 copy-done
  57.5 0.0 copy-start.2
  57.5 0.6 %copy.23 = f32[32,128]{1,0:T(8,128)} copy(f32[32,128]{1,0:T(8,128)S(1)} %copy-done) | data formatting | bytes 32768
  58.1 0.1 copy-done.2
  58.2 0.6 %copy.24 = f32[8,16]{1,0:T(8,128)} copy(f32[8,16]{1,0:T(8,128)S(1)} %copy-done.2) | data formatting | bytes 1024
Async XLA Ops:
  55.3 1.5 %copy-start.1 = (f32[32,128]{1,0:T(8,128)S(1)}, f32[32,128]{1,0:T(8,128)}, u32[]{:S(2)}) copy-start(f32[32,128]{1,0:T(8,128)} %get-tuple-element.17) | copy-start | bytes 49156
  56.8 0.7 %copy-start = (f32[32,128]{1,0:T(8,128)S(1)}, f32[32,128]{1,0:T(8,128)}, u32[]{:S(2)}) copy-start(f32[32,128]{1,0:T(8,128)} %get-tuple-element.18) | copy-start | bytes 49156
  57.5 0.7 %copy-start.2 = (f32[8,16]{1,0:T(8,128)S(1)}, f32[8,16]{1,0:T(8,128)}, u32[]{:S(2)}) copy-start(f32[8,16]{1,0:T(8,128)} %get-tuple-element.19) | copy-start | bytes 1540

commit v2 on v1

--- a/solution.py
+++ b/solution.py
@@ -64,11 +64,11 @@
 def kernel(
     atmos_in, wind_in, height_in, potential_in, neigh_in, coup_in,
     dsrc_in, dtgt_in, dwgt_in, usrc_in, utgt_in, uwgt_in, oper_in,
-    atmos_out, height_out, potential_out, flux_out,
+    result,
     atmos_v, wind_v, neigh_v, coup_v, dsrc_v, dtgt_v, dwgt_v, usrc_v, utgt_v, uwgt_v, oper_v,
     surf_h, tab_s, tab_r, edge_s, edge_r, oc0, oc_pack, oc_right, oc_left,
     mx0, mx_pack, mx_right, mx_left, g_s, g_r, h_s, u_r, part_v, wst_v,
-    aout_v, pout_v, fout_v, in_sem, out_sem, ssem, rsem,
+    in_sem, ssem, rsem,
 ):
     c = lax.axis_index("comp")
     t = lax.axis_index("tile")
@@ -81,6 +81,14 @@
     right = (t + 1) % NR
     left = (t + NR - 1) % NR
     own_q = k * 32 + r
+
+    wrap = lambda value, size: jnp.where(value >= size, value - size, value)
+    over_y = [wrap(y + i, 8) for i in (4, 5, 3, 6, 2, 7, 1, 0)]
+    over_z = [8 * wrap(z + i, 4) for i in (2, 1, 3, 0)]
+    chips = [zz + yy for yy in over_y for zz in over_z]
+    row_order = [2 * chip + kk for chip in chips for kk in (1 - k, k)]
+    peers = row_order[:-1]
+    peer_chips = [chip for chip in chips for _ in range(2)][:-1]
 
     def at(dc, dt):
         row = c if dc == 0 else (up_row if dc > 0 else down_row)
@@ -122,18 +130,11 @@
         if i != 0:
             greet(at(i, j))
 
-    def greet_far(i, carry):
+    for i in range(16):
         greet((up_row, i))
         greet((down_row, 48 + i))
-        return carry
-
-    lax.fori_loop(0, 16, greet_far, 0)
-
-    def greet_row(i, carry):
-        greet((c, (t + 1 + i) % NR))
-        return carry
-
-    lax.fori_loop(0, NR - 1, greet_row, 0)
+    for to in peers:
+        greet((c, to))
 
     lane8 = iota((8, 128), 1)
     last = jnp.where(lane8 == 127, 1.0, 0.0).astype(F32)
@@ -174,9 +175,6 @@
         send(s(32, 8), d(32, 8), which, at(0, -1))
         send(s(40, 8), d(40, 8), which, at(0, 1))
 
-    rate0 = rate_of(atmos)
-    stage_edges(0, rate0)
-
     loads[3].wait()
     loads[4].wait()
     band = iota((NR, 128), 0)
@@ -184,6 +182,20 @@
     tab_s[1] = (usrc_v[...] - 64 * band).astype(F32)
     for d in range(2):
         tab_r[d, pl.ds(own_q, 1)] = tab_s[d, pl.ds(t, 1)]
+
+    far = jnp.where((z == 0) | (z == 3), 1, 0)
+    pl.semaphore_wait(barrier, NR - 1 + 6 + NR * far)
+
+    centre = pl.ds(4, 1)
+    for i, j in around:
+        send(surf_h.at[:, centre], surf_h.at[:, pl.ds(4 - 3 * i - j, 1)], HALO, at(i, j))
+
+    for to in peers:
+        send(tab_s.at[:, pl.ds(to, 1)], tab_r.at[:, pl.ds(own_q, 1)], TABLE, (c, to))
+    rate0 = rate_of(atmos)
+    stage_edges(0, rate0)
+
+    send_edges(0)
 
     for i in (5, 6, 7, 8):
         loads[i].wait()
@@ -239,26 +251,6 @@
 
     oc_pack[...] = pack([oc0[f, own] for f in range(8)])
 
-    far = jnp.where((z == 0) | (z == 3), 1, 0)
-    pl.semaphore_wait(barrier, NR - 1 + 6 + NR * far)
-
-    centre = pl.ds(4, 1)
-    for i, j in around:
-        send(surf_h.at[:, centre], surf_h.at[:, pl.ds(4 - 3 * i - j, 1)], HALO, at(i, j))
-
-    def ordered(i):
-        j = i // 8
-        step_y = 4 + ((j + 1) // 2) * (2 * (j % 2) - 1)
-        zk = (i + 1) % 8
-        return ((z + zk // 2) % 4) * 16 + ((y + step_y) % 8) * 2 + (k + zk) % 2
-
-    def send_table(i, carry):
-        to = ordered(i)
-        send(tab_s.at[:, pl.ds(to, 1)], tab_r.at[:, pl.ds(own_q, 1)], TABLE, (c, to))
-        return carry
-
-    lax.fori_loop(0, NR - 1, send_table, 0)
-    send_edges(0)
     send_block(oc0, oc_pack, oc_right, oc_left, OCEAN)
 
     lane_s = iota((16, PTS), 1)
@@ -292,17 +284,12 @@
         row = jnp.where(z == 0, down_row, up_row)
         place = k * ROWS + jnp.where(z == 0, 32, 40) + y
 
-        def send_far(i, carry):
-            send(g_s.at[pl.ds(0, 1)], g_r.at[pl.ds(place, 1)], GATHER, (row, ordered(i)), FAR)
-            return carry
-
-        lax.fori_loop(0, NR, send_far, 0)
-
-    def send_surface(i, carry):
-        send(g_s.at[pl.ds(0, 1)], g_r.at[pl.ds(k * ROWS + r, 1)], GATHER, (c, ordered(i)))
-        return carry
-
-    lax.fori_loop(0, NR - 1, send_surface, 0)
+        for to in row_order:
+            send(g_s.at[pl.ds(0, 1)], g_r.at[pl.ds(place, 1)], GATHER, (row, to), FAR)
+
+    own_place = k * ROWS + r
+    for to in peers:
+        send(g_s.at[pl.ds(0, 1)], g_r.at[pl.ds(own_place, 1)], GATHER, (c, to))
 
     row_q = iota((NR, 128), 0)
     peer_q = 2 * (row_q % 32) + row_q // 32
@@ -403,9 +390,7 @@
         wst_v[i] = value if shift == 0 else roll(value, shift, 1)
 
     atmos = finish(1, atmos, rate1)
-    aout_v[...] = atmos
-    atmos_copy = pltpu.make_async_copy(aout_v, atmos_out, out_sem.at[0])
-    atmos_copy.start()
+    result[0:PTS] = atmos
 
     take_block(mx0, mx_right, mx_left, rsem, MATRIX)
     mx_rt, mx_lf = mx_right[...], mx_left[...]
@@ -440,17 +425,10 @@
     h_s[...] = height[0:OX, 0:OY]
     u_r[pl.ds(own_q, 1)] = h_s[pl.ds(r, 1)]
 
-    def send_height(i, carry):
-        to = ordered(i)
-        send(h_s.at[pl.ds(to // 2, 1)], u_r.at[pl.ds(own_q, 1)], UP, (c, to))
-        return carry
-
-    lax.fori_loop(0, NR - 1, send_height, 0)
-    pout_v[...] = potential[0:OX, 0:OY]
-    height_copy = pltpu.make_async_copy(h_s, height_out, out_sem.at[1])
-    potential_copy = pltpu.make_async_copy(pout_v, potential_out, out_sem.at[2])
-    height_copy.start()
-    potential_copy.start()
+    for to, chip in zip(peers, peer_chips):
+        send(h_s.at[pl.ds(chip, 1)], u_r.at[pl.ds(own_q, 1)], UP, (c, to))
+    result[PTS:PTS + OX] = height[0:OX, 0:OY]
+    result[PTS + OX:PTS + 2 * OX] = potential[0:OX, 0:OY]
 
     take(edge_r.at[0, pl.ds(0, 24)], ssem.at[HALO])
     take(tab_r.at[:, pl.ds(0, NR - 1)], ssem.at[TABLE])
@@ -474,11 +452,24 @@
         total = jnp.sum(up_cells[j] * cells, axis=1, keepdims=True)
         spread = spread + jnp.where(lane_64 == column0 + j, total, 0.0)
     flux = lax.dot_general(pick, spread, NN, precision=HIGHEST, preferred_element_type=F32)
-    fout_v[...] = flux[:, 0:AY]
-    flux_copy = pltpu.make_async_copy(fout_v, flux_out, out_sem.at[3])
-    flux_copy.start()
+    result[PTS + 2 * OX:PTS + 2 * OX + AX] = flux
     take(u_r.at[pl.ds(0, NR - 1)], ssem.at[UP])
-    for copy in (atmos_copy, height_copy, potential_copy, flux_copy):
+
+
+def hand_out(result, atmos_out, height_out, potential_out, flux_out, flux_v, sem):
+    flux_v[...] = result[PTS + 2 * OX:PTS + 2 * OX + AX, 0:AY]
+    copies = [
+        pltpu.make_async_copy(src, dst, sem.at[i])
+        for i, (src, dst) in enumerate([
+            (result.at[pl.ds(0, PTS)], atmos_out),
+            (result.at[pl.ds(PTS, OX)], height_out),
+            (result.at[pl.ds(PTS + OX, OX)], potential_out),
+            (flux_v, flux_out),
+        ])
+    ]
+    for copy in copies:
+        copy.start()
+    for copy in copies:
         copy.wait()
 
 
@@ -491,16 +482,12 @@
     any_spec = pl.BlockSpec(memory_space=pl.ANY)
     vm = lambda *shape, dtype=F32: pltpu.VMEM(shape, dtype)
     i32 = jnp.int32
-    outs = pl.pallas_call(
+    total_rows = PTS + 2 * OX + AX
+    packed = pl.pallas_call(
         kernel,
-        out_shape=[
-            jax.ShapeDtypeStruct((PTS, 128), F32),
-            jax.ShapeDtypeStruct((OX, OY), F32),
-            jax.ShapeDtypeStruct((OX, OY), F32),
-            jax.ShapeDtypeStruct((AX, AY), F32),
-        ],
+        out_shape=pltpu.VMEM((total_rows, 128), F32),
         in_specs=[any_spec] * 13,
-        out_specs=[any_spec] * 4,
+        out_specs=pl.BlockSpec(memory_space=pltpu.VMEM),
         scratch_shapes=[
             vm(PTS, 128), vm(2 * PTS, 128, dtype=jnp.bfloat16),
             vm(6, OX, OY, dtype=i32), vm(6, OX, OY),
@@ -512,8 +499,7 @@
             vm(2, ROWS, OY), vm(OX, OY), vm(ROWS, OY), vm(ROWS, OY),
             vm(8, 128), vm(2 * ROWS, 128), vm(OX, OY), vm(NR, 128),
             vm(2, NR, 128), vm(9, ROWS, 256),
-            vm(PTS, 128), vm(OX, OY), vm(AX, AY),
-            pltpu.SemaphoreType.DMA((13,)), pltpu.SemaphoreType.DMA((4,)),
+            pltpu.SemaphoreType.DMA((13,)),
             pltpu.SemaphoreType.DMA((13,)), pltpu.SemaphoreType.DMA((12,)),
         ],
         compiler_params=pltpu.CompilerParams(
@@ -527,6 +513,19 @@
         table(upward_source), table(upward_target), table(upward_weight),
         jnp.asarray(point_operators()),
     )
+    outs = pl.pallas_call(
+        hand_out,
+        out_shape=[
+            jax.ShapeDtypeStruct((PTS, 128), F32),
+            jax.ShapeDtypeStruct((OX, OY), F32),
+            jax.ShapeDtypeStruct((OX, OY), F32),
+            jax.ShapeDtypeStruct((AX, AY), F32),
+        ],
+        in_specs=[pl.BlockSpec(memory_space=pltpu.VMEM)],
+        out_specs=[any_spec] * 4,
+        scratch_shapes=[vm(AX, AY), pltpu.SemaphoreType.DMA((4,))],
+        name="hand_out",
+    )(pltpu.with_memory_space_constraint(packed, pltpu.VMEM))
     return (outs[0].reshape(AX, AY, 128), outs[1], outs[2], outs[3])
 
 

time: 59 us -> 50.1 us (0.85)
  Pallas kernels: 54.6 us -> 49.3 us
  local copies, waits for them, and re-layouts: 3.47 us -> 0 us
    pallas_call x1 -> x2, Pallas kernels: 54.6 us -> 49.3 us  [the longest x1 48.6 us: on_device(): pl.pallas_call(kernel, out_shape=pltpu.VMEM((total_rows, 128), F32), in_s...]
    unnamed x10 -> x0, local copies, waits for them, and re-layouts: 3.47 us -> none
where the time goes in v2:
time: 50.1 us; the launch traced here: 49.9 us
  Pallas kernels  49.3 us (98%)
  between operations  0.64 us (1%)
    pallas_call x1, Pallas kernels, on_device(): pl.pallas_call(kernel, out_shape=pltpu.VMEM((total_rows, 128), F32), in_s...  48.6 us

profile of v2, /device:TPU:1, one launch (start us, length us, event | category | flops | bytes accessed | tf_op | source)
XLA Modules:
  0.0 49.9 jit_solution(8120078872358435115)
XLA Ops:
  0.6 48.6 %coupled_step.1.result = f32[200,128]{1,0:T(8,128)S(1)} custom-call(f32[128,128]{1,0:T(8,128)} %bitcast.9, bf16[256,128]{1,0:T(8,128)(2,1)} %bitcast.10, f32[32,128]{1,0:T(8,128)} %height_in.1, f32[32,128]{1,0:T(8,128)} %potential_in.1, s32[6,32,128]{2,1,0:T(8,128)} %neigh_in.1, f32[6,32,128]{2,1,0:T(8,128)} %coup_in.1, s32[64,128]{1,0:T(8,128)} %bitcast.11, ...), custom_call_target="tpu_custom_call" | custom-call | tf_op jit(solution)/shard_map/coupled_step/pallas_call | solution.py:486
  49.2 0.7 %hand_out.1 = (f32[128,128]{1,0:T(8,128)}, f32[32,128]{1,0:T(8,128)}, f32[32,128]{1,0:T(8,128)}, f32[8,16]{1,0:T(8,128)}) custom-call(f32[200,128]{1,0:T(8,128)S(1)} %coupled_step.1.result), custom_call_target="tpu_custom_call" | custom-call | tf_op jit(solution)/shard_map/hand_out/pallas_call | solution.py:516

commit v3 on v2

--- a/solution.py
+++ b/solution.py
@@ -53,6 +53,13 @@
     return np.concatenate([curvature, along_x(first), along_y(first)]).astype(np.float32)
 
 
+def split_operators():
+    whole = point_operators()
+    high = whole.astype(jnp.bfloat16)
+    rest = (whole - high.astype(np.float32)).astype(jnp.bfloat16)
+    return np.concatenate([high, rest])
+
+
 def iota(shape, dim):
     return lax.broadcasted_iota(jnp.int32, shape, dim)
 
@@ -67,7 +74,7 @@
     result,
     atmos_v, wind_v, neigh_v, coup_v, dsrc_v, dtgt_v, dwgt_v, usrc_v, utgt_v, uwgt_v, oper_v,
     surf_h, tab_s, tab_r, edge_s, edge_r, oc0, oc_pack, oc_right, oc_left,
-    mx0, mx_pack, mx_right, mx_left, g_s, g_r, h_s, u_r, part_v, wst_v,
+    mx0, mx_pack, mx_right, mx_left, g_s, g_r, h_s, u_r, part_v, wst_v, pot_v,
     in_sem, ssem, rsem,
 ):
     c = lax.axis_index("comp")
@@ -76,8 +83,8 @@
     r = t // 2
     z = t // 16
     y = (t // 2) % 8
-    up_row = (c + 1) % NC
-    down_row = (c + NC - 1) % NC
+    comp_at = lambda i: (c + i + NC) % NC
+    comps = {i: comp_at(i) for i in (-1, 0, 1)}
     right = (t + 1) % NR
     left = (t + NR - 1) % NR
     own_q = k * 32 + r
@@ -91,11 +98,11 @@
     peer_chips = [chip for chip in chips for _ in range(2)][:-1]
 
     def at(dc, dt):
-        row = c if dc == 0 else (up_row if dc > 0 else down_row)
+        row = comps[dc]
         col = t if dt == 0 else (right if dt > 0 else left)
         return (row, col)
 
-    around = [(i, j) for i in (-1, 0, 1) for j in (-1, 0, 1) if (i, j) != (0, 0)]
+    around = [(i, j) for i in (-1, 1, 0) for j in (-1, 1, 0) if (i, j) != (0, 0)]
 
     def send(src, dst, which, to, left_by=None):
         pltpu.make_async_remote_copy(
@@ -107,13 +114,25 @@
     def take(ref, sem):
         pltpu.make_async_copy(ref, ref, sem).wait()
 
+    barrier = pltpu.get_barrier_semaphore()
+
+    def greet(to):
+        pl.semaphore_signal(barrier, inc=1, device_id=to, device_id_type=MESH)
+
+
+    for i in range(16):
+        greet((comps[1], i))
+        greet((comps[-1], 48 + i))
+    for i, j in around:
+        if i != 0:
+            greet(at(i, j))
     loads = [
         pltpu.make_async_copy(src, dst, in_sem.at[i])
         for i, (src, dst) in enumerate([
             (atmos_in, atmos_v), (oper_in, oper_v), (wind_in, wind_v),
             (dsrc_in, dsrc_v), (usrc_in, usrc_v),
             (neigh_in, neigh_v), (coup_in, coup_v),
-            (height_in, oc0.at[0, pl.ds(0, OX)]), (potential_in, oc0.at[1, pl.ds(0, OX)]),
+            (height_in, oc0.at[0, pl.ds(8, OX)]), (potential_in, oc0.at[1, pl.ds(8, OX)]),
             (dtgt_in, dtgt_v), (dwgt_in, dwgt_v), (utgt_in, utgt_v), (uwgt_in, uwgt_v),
         ])
     ]
@@ -121,38 +140,36 @@
         load.start()
     surf_h[:, 9:16, :] = jnp.zeros((3, 7, PTS), F32)
 
-    barrier = pltpu.get_barrier_semaphore()
-
-    def greet(to):
-        pl.semaphore_signal(barrier, inc=1, device_id=to, device_id_type=MESH)
-
-    for i, j in around:
-        if i != 0:
-            greet(at(i, j))
-
-    for i in range(16):
-        greet((up_row, i))
-        greet((down_row, 48 + i))
+
     for to in peers:
         greet((c, to))
 
-    lane8 = iota((8, 128), 1)
-    last = jnp.where(lane8 == 127, 1.0, 0.0).astype(F32)
-    pick_last = lambda block: lax.dot_general(
-        last, block, NT, precision=HIGHEST, preferred_element_type=F32
-    )[0:1]
+    last = jnp.where(iota((16, 128), 1) == 127, 1.0, 0.0).astype(F32)
     loads[0].wait()
-    loads[1].wait()
     loads[2].wait()
     atmos = atmos_v[...]
+    surf_h[0, 4:5] = lax.dot_general(
+        last[0:8], atmos, NT, precision=HIGHEST, preferred_element_type=F32
+    )[0:1]
+    winds = lax.dot_general(
+        last.astype(jnp.bfloat16), wind_v[...], NT, preferred_element_type=F32
+    )[0:1]
+    surf_h[1, 4:5] = winds[:, 0:PTS]
+    surf_h[2, 4:5] = winds[:, PTS:2 * PTS]
     east = wind_v[0:PTS].astype(F32)
     north = wind_v[PTS:2 * PTS].astype(F32)
-    surf_h[0, 4:5] = pick_last(atmos)
-    surf_h[1, 4:5] = pick_last(east)
-    surf_h[2, 4:5] = pick_last(north)
+
+    def parts(value):
+        high = value.astype(jnp.bfloat16)
+        return high, (value - high.astype(F32)).astype(jnp.bfloat16)
+
+    def product(lhs, rhs, dims):
+        return lax.dot_general(lhs, rhs, dims, preferred_element_type=F32)
 
     def rate_of(a):
-        res = lax.dot_general(oper_v[...], a, NN, precision=HIGHEST, preferred_element_type=F32)
+        high, low = parts(a)
+        both = product(oper_v[...], high, NN)
+        res = both[0:3 * PTS] + (both[3 * PTS:6 * PTS] + product(oper_v[0:3 * PTS], low, NN))
         return res[0:PTS] - (east * res[PTS:2 * PTS] + north * res[2 * PTS:3 * PTS])
 
     def stage_edges(step, rate):
@@ -192,6 +209,7 @@
 
     for to in peers:
         send(tab_s.at[:, pl.ds(to, 1)], tab_r.at[:, pl.ds(own_q, 1)], TABLE, (c, to))
+    loads[1].wait()
     rate0 = rate_of(atmos)
     stage_edges(0, rate0)
 
@@ -209,7 +227,7 @@
             total = total + jnp.where(place == code, coef, 0.0)
         return total
 
-    own = slice(0, OX)
+    own = slice(8, 8 + OX)
     oc0[2, own] = weight_of(-1, 0)
     oc0[3, own] = weight_of(1, 0)
     oc0[4, own] = weight_of(0, -1)
@@ -228,17 +246,18 @@
 
     def send_block(full, packed, rt, lf, which):
         top, bottom = pl.ds(0, 8), pl.ds(24, 8)
-        send(full.at[:, bottom], full.at[:, pl.ds(40, 8)], which, at(1, 0))
-        send(full.at[:, top], full.at[:, pl.ds(32, 8)], which, at(-1, 0))
-        send(packed.at[bottom], rt.at[pl.ds(40, 8)], which + 1, at(1, -1))
-        send(packed.at[top], rt.at[pl.ds(32, 8)], which + 1, at(-1, -1))
-        send(packed, rt.at[pl.ds(0, OX)], which + 1, at(0, -1))
-        send(packed.at[bottom], lf.at[pl.ds(40, 8)], which + 2, at(1, 1))
-        send(packed.at[top], lf.at[pl.ds(32, 8)], which + 2, at(-1, 1))
-        send(packed, lf.at[pl.ds(0, OX)], which + 2, at(0, 1))
+        above, below, beside = pl.ds(0, 8), pl.ds(8 + OX, 8), pl.ds(8, OX)
+        send(full.at[:, pl.ds(OX, 8)], full.at[:, above], which, at(1, 0))
+        send(full.at[:, pl.ds(8, 8)], full.at[:, below], which, at(-1, 0))
+        send(packed.at[bottom], rt.at[above], which + 1, at(1, -1))
+        send(packed.at[top], rt.at[below], which + 1, at(-1, -1))
+        send(packed, rt.at[beside], which + 1, at(0, -1))
+        send(packed.at[bottom], lf.at[above], which + 2, at(1, 1))
+        send(packed.at[top], lf.at[below], which + 2, at(-1, 1))
+        send(packed, lf.at[beside], which + 2, at(0, 1))
 
     def take_block(full, rt, lf, sems, which):
-        take(full.at[:, pl.ds(32, 16)], sems.at[which])
+        take(full.at[:, pl.ds(0, 16)], sems.at[which])
         take(rt, sems.at[which + 1])
         take(lf, sems.at[which + 2])
 
@@ -266,7 +285,9 @@
     surf_e = surf_h[1]
     surf_n = surf_h[2]
     for _ in range(SUBSTEPS):
-        res = lax.dot_general(surf, oper_v[...], NT, precision=HIGHEST, preferred_element_type=F32)
+        high, low = parts(surf)
+        both = product(jnp.concatenate([high, low], axis=0), oper_v[0:3 * PTS], NT)
+        res = both[0:16] + (both[16:32] + product(high, oper_v[3 * PTS:6 * PTS], NT))
         rate = res[:, 0:PTS] - (surf_e * res[:, PTS:2 * PTS] + surf_n * res[:, 2 * PTS:3 * PTS])
         nxt, prv = roll(rate, -16, 1), roll(rate, 16, 1)
         after = jnp.where(xs == AX - 1, roll(nxt, -3, 0), nxt)
@@ -275,21 +296,19 @@
         after = jnp.where(ys == AY - 1, roll(roll(rate, 15, 1), -1, 0), roll(rate, -1, 1))
         before = jnp.where(ys == 0, roll(roll(rate, -15, 1), 1, 0), roll(rate, 1, 1))
         surf = surf + atmos_step * pairs(rate, after, before, ys % 4)
-    surf_row = surf[4:5]
-    g_s[0:1] = surf_row
-    g_r[pl.ds(k * ROWS + r, 1)] = surf_row
+    g_s[0:1] = surf[4:5]
+    mine = pl.ds(k * ROWS + 8 + r, 1)
+    g_r[mine] = g_s[0:1]
 
     @pl.when(far == 1)
     def _():
-        row = jnp.where(z == 0, down_row, up_row)
-        place = k * ROWS + jnp.where(z == 0, 32, 40) + y
-
+        row = jnp.where(z == 0, comps[-1], comps[1])
+        place = pl.ds(k * ROWS + jnp.where(z == 0, 8 + OX, 0) + y, 1)
         for to in row_order:
-            send(g_s.at[pl.ds(0, 1)], g_r.at[pl.ds(place, 1)], GATHER, (row, to), FAR)
-
-    own_place = k * ROWS + r
+            send(g_s.at[pl.ds(0, 1)], g_r.at[place], GATHER, (row, to), FAR)
+
     for to in peers:
-        send(g_s.at[pl.ds(0, 1)], g_r.at[pl.ds(own_place, 1)], GATHER, (c, to))
+        send(g_s.at[pl.ds(0, 1)], g_r.at[mine], GATHER, (c, to))
 
     row_q = iota((NR, 128), 0)
     peer_q = 2 * (row_q % 32) + row_q // 32
@@ -362,6 +381,90 @@
     stage_edges(1, rate1)
     send_edges(1)
 
+    take_block(oc0, oc_right, oc_left, rsem, OCEAN)
+    oc_rt, oc_lf = oc_right[...], oc_left[...]
+    wide = [(oc0[f], beside(oc_rt, oc_lf, f)) for f in range(8)]
+
+    def shifted(pair, step):
+        a, b = (roll(v, step, 1) for v in pair)
+        edge = lane_x == (0 if step == 1 else OY - 1)
+        return jnp.where(edge, b, a), jnp.where(edge, a, b)
+
+    height, potential = list(wide[0]), list(wide[1])
+    w_n, w_s, w_w, w_e, pair_s, pair_n = [
+        tuple(ocean_step * v for v in pair) for pair in wide[2:]
+    ]
+    positive = lambda pair: tuple(jnp.maximum(v, 0.0) for v in pair)
+    negative = lambda pair: tuple(jnp.maximum(-v, 0.0) for v in pair)
+    w_se, w_sw = positive(pair_s), negative(pair_s)
+    w_nw, w_ne = positive(pair_n), negative(pair_n)
+    w_c = tuple(
+        -(n + s + w + e + abs(ps) + abs(pn))
+        for n, s, w, e, ps, pn in zip(w_n, w_s, w_w, w_e, pair_s, pair_n)
+    )
+    for i, (value, shift) in enumerate([
+        (w_nw, -1), (w_w, -1), (w_sw, -1),
+        (w_n, 0), (w_c, 0), (w_s, 0),
+        (w_ne, 1), (w_e, 1), (w_se, 1),
+    ]):
+        value = value if shift == 0 else shifted(value, shift)
+        for half in range(2):
+            wst_v[i, half] = value[half]
+    for half in range(2):
+        pot_v[half, 0:8] = jnp.zeros((8, OY), F32)
+        pot_v[half, 8 + ROWS:16 + ROWS] = jnp.zeros((8, OY), F32)
+
+    take_block(mx0, mx_right, mx_left, rsem, MATRIX)
+    mx_rt, mx_lf = mx_right[...], mx_left[...]
+    mx1 = [beside(mx_rt, mx_lf, j) for j in range(2)]
+    take(g_r.at[pl.ds(0, 95)], rsem.at[GATHER])
+    even, odd = g_r[0:ROWS], g_r[ROWS:2 * ROWS]
+
+    def column_of(block, point):
+        return jnp.sum(jnp.where(lane_x == point, block, 0.0), axis=1, keepdims=True)
+
+    near = jnp.zeros((ROWS, OY), F32)
+    side = jnp.zeros((ROWS, OY), F32)
+    for j in range(2):
+        here = jnp.where(lane_x < 64, column_of(even, 2 * t + j), column_of(odd, 2 * t + j))
+        there = jnp.where(
+            lane_x < 64, column_of(even, 2 * right + j), column_of(odd, 2 * left + j)
+        )
+        near = near + mx0[j] * here
+        side = side + mx1[j] * there
+    forcing = (ocean_step * near, ocean_step * side)
+
+    for _ in range(SUBCYCLES):
+        for half in range(2):
+            potential[half] = (
+                (1.0 - friction) * potential[half]
+                + ((ocean_step * wave_speed) * height[half] + forcing[half])
+            )
+            pot_v[half, 8:8 + ROWS] = potential[half]
+        sums = [[], [], []]
+        for half in range(2):
+            above = pot_v[half, 7:7 + ROWS]
+            below = pot_v[half, 9:9 + ROWS]
+            for j in range(3):
+                sums[j].append(
+                    wst_v[3 * j, half] * above
+                    + wst_v[3 * j + 1, half] * potential[half]
+                    + wst_v[3 * j + 2, half] * below
+                )
+        west, east_sum = shifted(sums[0], 1), shifted(sums[2], -1)
+        for half in range(2):
+            height[half] = (height[half] + sums[1][half]) + (west[half] + east_sum[half])
+
+    h_s[...] = height[0][own]
+    u_r[pl.ds(own_q, 1)] = h_s[pl.ds(r, 1)]
+    for to, chip in zip(peers, peer_chips):
+        send(h_s.at[pl.ds(chip, 1)], u_r.at[pl.ds(own_q, 1)], UP, (c, to))
+    result[PTS:PTS + OX] = height[0][own]
+    result[PTS + OX:PTS + 2 * OX] = potential[0][own]
+
+    atmos = finish(1, atmos, rate1)
+    result[0:PTS] = atmos
+
     for i in (11, 12):
         loads[i].wait()
     upward = matrices(
@@ -373,62 +476,6 @@
         low = jnp.where(k == 0, upward[j], blank)
         high = jnp.where(k == 0, blank, upward[j])
         up_cells.append(jnp.concatenate([low, high], axis=0).T[0:NR])
-
-    take_block(oc0, oc_right, oc_left, rsem, OCEAN)
-    oc_rt, oc_lf = oc_right[...], oc_left[...]
-    wide = [jnp.concatenate([oc0[f], beside(oc_rt, oc_lf, f)], axis=1) for f in range(8)]
-    height, potential, w_n, w_s, w_w, w_e, pair_s, pair_n = wide
-    w_se, w_sw = jnp.maximum(pair_s, 0.0), jnp.maximum(-pair_s, 0.0)
-    w_nw, w_ne = jnp.maximum(pair_n, 0.0), jnp.maximum(-pair_n, 0.0)
-    w_c = -(w_n + w_s + w_w + w_e + w_se + w_sw + w_nw + w_ne)
-    for i, (value, shift) in enumerate([
-        (w_nw, -1), (w_w, -1), (w_sw, -1),
-        (w_n, 0), (w_c, 0), (w_s, 0),
-        (w_ne, 1), (w_e, 1), (w_se, 1),
-    ]):
-        value = ocean_step * value
-        wst_v[i] = value if shift == 0 else roll(value, shift, 1)
-
-    atmos = finish(1, atmos, rate1)
-    result[0:PTS] = atmos
-
-    take_block(mx0, mx_right, mx_left, rsem, MATRIX)
-    mx_rt, mx_lf = mx_right[...], mx_left[...]
-    mx1 = [beside(mx_rt, mx_lf, j) for j in range(2)]
-    take(g_r.at[pl.ds(0, 95)], rsem.at[GATHER])
-    even, odd = g_r[0:ROWS], g_r[ROWS:2 * ROWS]
-
-    def column_of(block, point):
-        return jnp.sum(jnp.where(lane_x == point, block, 0.0), axis=1, keepdims=True)
-
-    near = jnp.zeros((ROWS, OY), F32)
-    side = jnp.zeros((ROWS, OY), F32)
-    for j in range(2):
-        here = jnp.where(lane_x < 64, column_of(even, 2 * t + j), column_of(odd, 2 * t + j))
-        there = jnp.where(
-            lane_x < 64, column_of(even, 2 * right + j), column_of(odd, 2 * left + j)
-        )
-        near = near + mx0[j] * here
-        side = side + mx1[j] * there
-    forcing = ocean_step * jnp.concatenate([near, side], axis=1)
-
-    for _ in range(SUBCYCLES):
-        potential = (1.0 - friction) * potential + (ocean_step * wave_speed) * height + forcing
-        above = roll(potential, 1, 0)
-        below = roll(potential, -1, 0)
-        sums = [
-            wst_v[3 * j] * above + wst_v[3 * j + 1] * potential + wst_v[3 * j + 2] * below
-            for j in range(3)
-        ]
-        height = height + sums[1] + roll(sums[0], 1, 1) + roll(sums[2], -1, 1)
-
-    h_s[...] = height[0:OX, 0:OY]
-    u_r[pl.ds(own_q, 1)] = h_s[pl.ds(r, 1)]
-
-    for to, chip in zip(peers, peer_chips):
-        send(h_s.at[pl.ds(chip, 1)], u_r.at[pl.ds(own_q, 1)], UP, (c, to))
-    result[PTS:PTS + OX] = height[0:OX, 0:OY]
-    result[PTS + OX:PTS + 2 * OX] = potential[0:OX, 0:OY]
 
     take(edge_r.at[0, pl.ds(0, 24)], ssem.at[HALO])
     take(tab_r.at[:, pl.ds(0, NR - 1)], ssem.at[TABLE])
@@ -493,12 +540,12 @@
             vm(6, OX, OY, dtype=i32), vm(6, OX, OY),
             vm(NR, 128, dtype=i32), vm(NR, 128, dtype=i32), vm(NR, 128),
             vm(NR, 128, dtype=i32), vm(NR, 128, dtype=i32), vm(NR, 128),
-            vm(3 * PTS, PTS),
+            vm(6 * PTS, PTS, dtype=jnp.bfloat16),
             vm(3, 16, PTS), vm(2, NR, 128), vm(2, NR, 128), vm(2, 48, 128), vm(2, 56, 128),
             vm(8, ROWS, OY), vm(OX, OY), vm(ROWS, OY), vm(ROWS, OY),
             vm(2, ROWS, OY), vm(OX, OY), vm(ROWS, OY), vm(ROWS, OY),
             vm(8, 128), vm(2 * ROWS, 128), vm(OX, OY), vm(NR, 128),
-            vm(2, NR, 128), vm(9, ROWS, 256),
+            vm(2, NR, 128), vm(9, 2, ROWS, OY), vm(2, ROWS + 16, OY),
             pltpu.SemaphoreType.DMA((13,)),
             pltpu.SemaphoreType.DMA((13,)), pltpu.SemaphoreType.DMA((12,)),
         ],
@@ -511,7 +558,7 @@
         ocean_height, ocean_potential, ocean_neighbors, ocean_coupling,
         table(downward_source), table(downward_target), table(downward_weight),
         table(upward_source), table(upward_target), table(upward_weight),
-        jnp.asarray(point_operators()),
+        jnp.asarray(split_operators()),
     )
     outs = pl.pallas_call(
         hand_out,

time: 50.1 us -> 49.3 us (0.984)
  Pallas kernels: 49.3 us -> 48.5 us
    pallas_call x1, Pallas kernels: 48.6 us -> 47.9 us  [on_device(): pl.pallas_call(kernel, out_shape=pltpu.VMEM((total_rows, 128), F32), in_s...]
where the time goes in v3:
time: 49.3 us; the launch traced here: 49.2 us
  Pallas kernels  48.5 us (98%)
  between operations  0.64 us (1%)
    pallas_call x1, Pallas kernels, on_device(): pl.pallas_call(kernel, out_shape=pltpu.VMEM((total_rows, 128), F32), in_s...  47.9 us

profile of v3, /device:TPU:1, one launch (start us, length us, event | category | flops | bytes accessed | tf_op | source)
XLA Modules:
  0.0 49.2 jit_solution(18258224306747825163)
XLA Ops:
  0.6 47.9 %coupled_step.1.result = f32[200,128]{1,0:T(8,128)S(1)} custom-call(f32[128,128]{1,0:T(8,128)} %bitcast.9, bf16[256,128]{1,0:T(8,128)(2,1)} %bitcast.10, f32[32,128]{1,0:T(8,128)} %height_in.1, f32[32,128]{1,0:T(8,128)} %potential_in.1, s32[6,32,128]{2,1,0:T(8,128)} %neigh_in.1, f32[6,32,128]{2,1,0:T(8,128)} %coup_in.1, s32[64,128]{1,0:T(8,128)} %bitcast.11, ...), custom_call_target="tpu_custom_call" | custom-call | tf_op jit(solution)/shard_map/coupled_step/pallas_call | solution.py:533
  48.5 0.7 %hand_out.1 = (f32[128,128]{1,0:T(8,128)}, f32[32,128]{1,0:T(8,128)}, f32[32,128]{1,0:T(8,128)}, f32[8,16]{1,0:T(8,128)}) custom-call(f32[200,128]{1,0:T(8,128)S(1)} %coupled_step.1.result), custom_call_target="tpu_custom_call" | custom-call | tf_op jit(solution)/shard_map/hand_out/pallas_call | solution.py:563

commit v4 on v3

--- a/solution.py
+++ b/solution.py
@@ -27,7 +27,7 @@
 wave_speed = 1.0
 friction = 0.05
 
-HALO, TABLE, EDGE, OCEAN, MATRIX, GATHER, UP, FAR = 0, 1, 2, 4, 7, 10, 11, 12
+HALO, TABLE, EDGE, OCEAN, MATRIX, GATHER, UP, TABLE_UP, FAR = 0, 1, 2, 4, 7, 10, 11, 12, 13
 
 
 def gll_derivative():
@@ -208,7 +208,7 @@
         send(surf_h.at[:, centre], surf_h.at[:, pl.ds(4 - 3 * i - j, 1)], HALO, at(i, j))
 
     for to in peers:
-        send(tab_s.at[:, pl.ds(to, 1)], tab_r.at[:, pl.ds(own_q, 1)], TABLE, (c, to))
+        send(tab_s.at[0, pl.ds(to, 1)], tab_r.at[0, pl.ds(own_q, 1)], TABLE, (c, to))
     loads[1].wait()
     rate0 = rate_of(atmos)
     stage_edges(0, rate0)
@@ -342,7 +342,7 @@
 
     for i in (9, 10):
         loads[i].wait()
-    take(tab_r.at[:, pl.ds(0, NR - 1)], rsem.at[TABLE])
+    take(tab_r.at[0, pl.ds(0, NR - 1)], rsem.at[TABLE])
     down = matrices(
         (by_core(dtgt_v) - 64 * peer_q).astype(F32), tab_r[0], by_core(dwgt_v)
     )
@@ -376,6 +376,8 @@
         before = jnp.where(ya == 0, west_col, roll(across, 1, 0))
         return a + atmos_step * pairs(across, after, before, ya % 4)
 
+    for to in peers:
+        send(tab_s.at[1, pl.ds(to, 1)], tab_r.at[1, pl.ds(own_q, 1)], TABLE_UP, (c, to))
     atmos = finish(0, atmos, rate0)
     rate1 = rate_of(atmos)
     stage_edges(1, rate1)
@@ -467,6 +469,7 @@
 
     for i in (11, 12):
         loads[i].wait()
+    take(tab_r.at[1, pl.ds(0, NR - 1)], rsem.at[TABLE_UP])
     upward = matrices(
         tab_r[1], (by_core(utgt_v) - 2 * peer_q).astype(F32), by_core(uwgt_v)
     )
@@ -478,7 +481,8 @@
         up_cells.append(jnp.concatenate([low, high], axis=0).T[0:NR])
 
     take(edge_r.at[0, pl.ds(0, 24)], ssem.at[HALO])
-    take(tab_r.at[:, pl.ds(0, NR - 1)], ssem.at[TABLE])
+    take(tab_r.at[0, pl.ds(0, NR - 1)], ssem.at[TABLE])
+    take(tab_r.at[1, pl.ds(0, NR - 1)], ssem.at[TABLE_UP])
     take(edge_r.at[0, pl.ds(0, 52)], ssem.at[EDGE])
     take(edge_r.at[1, pl.ds(0, 52)], ssem.at[EDGE + 1])
     take_block(oc0, oc_right, oc_left, ssem, OCEAN)
@@ -547,7 +551,7 @@
             vm(8, 128), vm(2 * ROWS, 128), vm(OX, OY), vm(NR, 128),
             vm(2, NR, 128), vm(9, 2, ROWS, OY), vm(2, ROWS + 16, OY),
             pltpu.SemaphoreType.DMA((13,)),
-            pltpu.SemaphoreType.DMA((13,)), pltpu.SemaphoreType.DMA((12,)),
+            pltpu.SemaphoreType.DMA((14,)), pltpu.SemaphoreType.DMA((13,)),
         ],
         compiler_params=pltpu.CompilerParams(
             collective_id=0, has_side_effects=True, vmem_limit_bytes=60 * 1024 * 1024

time: 49.3 us -> 49.4 us (level)
  no operation moved by 1% of the time
where the time goes in v4:
time: 49.4 us; the launch traced here: 49.3 us
  Pallas kernels  48.6 us (98%)
  between operations  0.64 us (1%)
    pallas_call x1, Pallas kernels, on_device(): pl.pallas_call(kernel, out_shape=pltpu.VMEM((total_rows, 128), F32), in_s...  48 us

profile of v4, /device:TPU:1, one launch (start us, length us, event | category | flops | bytes accessed | tf_op | source)
XLA Modules:
  0.0 49.3 jit_solution(1109480163577215180)
XLA Ops:
  0.6 48.0 %coupled_step.1.result = f32[200,128]{1,0:T(8,128)S(1)} custom-call(f32[128,128]{1,0:T(8,128)} %bitcast.9, bf16[256,128]{1,0:T(8,128)(2,1)} %bitcast.10, f32[32,128]{1,0:T(8,128)} %height_in.1, f32[32,128]{1,0:T(8,128)} %potential_in.1, s32[6,32,128]{2,1,0:T(8,128)} %neigh_in.1, f32[6,32,128]{2,1,0:T(8,128)} %coup_in.1, s32[64,128]{1,0:T(8,128)} %bitcast.11, ...), custom_call_target="tpu_custom_call" | custom-call | tf_op jit(solution)/shard_map/coupled_step/pallas_call | solution.py:537
  48.6 0.7 %hand_out.1 = (f32[128,128]{1,0:T(8,128)}, f32[32,128]{1,0:T(8,128)}, f32[32,128]{1,0:T(8,128)}, f32[8,16]{1,0:T(8,128)}) custom-call(f32[200,128]{1,0:T(8,128)S(1)} %coupled_step.1.result), custom_call_target="tpu_custom_call" | custom-call | tf_op jit(solution)/shard_map/hand_out/pallas_call | solution.py:567
